TPU v7x, 512 devices: a whole 4x8x8 slice. The times are simulated.
512 devices in a mesh: dp: 64 (over x, y_hi, z), expert: 4 (over y_lo), tensor: 2 (over core).
Axes of the slice: x: 4, y: 8 (y_hi: 2, y_lo: 4; y = y_hi * 4 + y_lo), z: 8, core: 2. Of those that a mesh axis runs over, the one named last changes fastest.
Arguments:
- saved_rows: bfloat16 [64, 4, 512, 6144], P('dp', 'expert', None, 'tensor'), may hold values from -6 to 6
- grad_hidden: bfloat16 [64, 4, 128, 512], P('dp', 'expert', 'tensor'), may hold values from -0.15625 to 0.15625
- counts: int32 [64, 8], P('dp', 'expert'), may hold values from 1 to 256, as said below
- offsets: int32 [64, 8], P('dp', 'expert'), may hold values from 0 to 256, as said below
- master: float32 [8, 2, 64, 6144], P('expert', 'tensor', 'dp'), may hold values from -1.2 to 1.2
- moment1: float32 [8, 2, 64, 6144], P('expert', 'tensor', 'dp'), may hold values from -3 to 3
- moment2: float32 [8, 2, 64, 6144], P('expert', 'tensor', 'dp'), may hold values from 0.25 to 4
- next_rows: bfloat16 [64, 8, 64, 6144], P('dp', 'expert', None, 'tensor'), may hold values from -6 to 6
Outputs:
- new_master: float32 [8, 2, 64, 6144], P('expert', 'tensor', 'dp')
- new_moment1: float32 [8, 2, 64, 6144], P('expert', 'tensor', 'dp')
- new_moment2: float32 [8, 2, 64, 6144], P('expert', 'tensor', 'dp')
- next_gate: float32 [64, 8, 128, 64], P('dp', 'expert', 'tensor')
Inputs may be any that keep to these rules, and one draw needn't show every extreme that they name: `counts`: on every index of dp some expert has exactly 256 rows. On each buffer the experts' rows do not intersect, the first expert's before the second's, and offsets + 256 <= 512; in every draw some buffer's second expert begins at row 256.
All inputs are finite; a program needn't handle non-finite values.
Results may differ from a plain program's by a relative error of at most 0.0029.
Values may be sent and summed in bfloat16 or wider, within the bound.
No kernel may reach another device: no remote copies, remote signals or barrier semaphores. Data moves between devices by JAX's collectives and lax.ppermute only.
A program may use at most 64 MiB of HBM per device.

v0:
```python
import jax
import jax.numpy as jnp
from jax import lax
from jax.sharding import PartitionSpec as P

first_decay = 0.9
second_decay = 0.95
first_fix = 1.0 - 0.9**11
second_fix = 1.0 - 0.95**11
learn_rate = 0.01
weight_decay = 0.1
adam_epsilon = 1e-08


def adamw(grad, weight, first, second):
    new_first = first_decay * first + (1.0 - first_decay) * grad
    new_second = second_decay * second + (1.0 - second_decay) * grad * grad
    update = (
        new_first / first_fix / (jnp.sqrt(new_second / second_fix) + adam_epsilon)
        + weight_decay * weight
    )
    return (weight - learn_rate * update, new_first, new_second)


def row_products(hidden, starts, sizes, row_total):
    line = jnp.arange(row_total, dtype=jnp.int32)
    inside = (
        (line[None, :] >= starts[:, None]) & (line[None, :] < (starts + sizes)[:, None])
    ).astype(jnp.bfloat16)
    masked = hidden[None, :, :] * inside[:, None, :]

    def partial_grad(piece, start):
        return jnp.einsum("ebr,rk->ebk", masked, piece, preferred_element_type=jnp.float32)

    return partial_grad


def per_device(saved_rows, grad_hidden, counts, offsets, master, moment1, moment2, next_rows):
    row_total = saved_rows.shape[2]
    starts = offsets[0]
    sizes = counts[0]
    partial_grad = row_products(grad_hidden[0, 0], starts, sizes, row_total)
    grad = partial_grad(
        lax.all_gather(saved_rows, "tensor", axis=3, tiled=True)[0, 0], jnp.int32(0)
    )[:, None]
    inputs = lax.all_gather(next_rows, "tensor", axis=3, tiled=True)[0]
    summed = lax.psum_scatter(grad, "dp", scatter_dimension=2, tiled=True)
    new_master, new_moment1, new_moment2 = adamw(summed, master, moment1, moment2)
    weights = new_master.astype(jnp.bfloat16)
    scale = master.shape[3] ** (-0.5)
    gates = jnp.einsum(
        "etkd,end->etkn",
        lax.all_gather(weights, "dp", axis=2, tiled=True),
        inputs,
        preferred_element_type=jnp.float32,
    )
    gates = gates.reshape(gates.shape[0], gates.shape[1] * gates.shape[2], gates.shape[3])
    next_gate = gates * scale
    return (new_master, new_moment1, new_moment2, next_gate[None])


def solution(mesh):
    placed = (
        P("dp", "expert", None, "tensor"),
        P("dp", "expert", "tensor", None),
        P("dp", "expert"),
        P("dp", "expert"),
        P("expert", "tensor", "dp", None),
        P("expert", "tensor", "dp", None),
        P("expert", "tensor", "dp", None),
        P("dp", "expert", None, "tensor"),
    )
    return jax.shard_map(
        per_device,
        mesh=mesh,
        in_specs=placed,
        out_specs=(
            P("expert", "tensor", "dp", None),
            P("expert", "tensor", "dp", None),
            P("expert", "tensor", "dp", None),
            P("dp", "expert", "tensor", None),
        ),
        check_vma=False,
    )
```

profile of v0, /device:TPU:8, one launch (start us, length us, event | category | flops | bytes accessed | tf_op | source)
XLA Modules:
  0.0 1067.2 jit_solution(3277815799851987830)
XLA Ops:
  7.2 0.0 all-gather.4.cloned.1.call-start
  7.2 0.7 all-gather.4.cloned.1.call-update
  7.9 0.0 all-reduce.3.cloned.1.call-start
  8.0 0.1 and_convert_fusion
  8.1 31.5 %all-gather.4.cloned.1.call-done = bf16[1,1,512,6144]{3,2,1,0:T(8,128)(2,1)} async-done(((bf16[1,1,512,3072]{3,2,1,0:T(8,128)(2,1)}), bf16[1,1,512,6144]{3,2,1,0:T(8,128)(2,1)}) %all-gather.4.cloned.1.call-update) | async-done | bytes 6291472 | tf_op jit(solution)/shard_map/all_gather | solution.py:44
  39.6 0.0 copy-done
  39.6 3.8 convolution_bitcast_fusion
  43.4 4.1 copy.23
  47.5 0.0 all-reduce.3.cloned.1.call-update
  47.5 0.0 all-gather.8.cloned.1.call-start
  47.6 0.7 all-gather.8.cloned.1.call-update
  48.3 0.0 all-gather.6.cloned.1.call-start
  48.3 1.3 dynamic-slice
  49.6 850.6 %all-reduce.3.cloned.1.call-done = f32[2,1,64,6144]{3,0,1,2:T(2,128)} async-done(((f32[2,1,64,6144]{3,0,1,2:T(2,128)}), f32[2,1,64,6144]{3,0,1,2:T(2,128)}) %all-reduce.3.cloned.1.call-update) | async-done | bytes 3145744
  900.2 0.0 copy-done.1
  900.2 0.0 copy-done.3
  900.2 2.2 fusion.20
  902.5 0.0 all-gather.6.cloned.1.call-update
  902.5 0.7 copy.28
  903.2 0.7 copy.29
  903.8 0.7 copy.30
  904.5 14.0 %all-gather.8.cloned.1.call-done = bf16[1,2,64,6144]{3,2,1,0:T(8,128)(2,1)} async-done(((bf16[1,2,64,3072]{3,2,1,0:T(8,128)(2,1)}), bf16[1,2,64,6144]{3,2,1,0:T(8,128)(2,1)}) %all-gather.8.cloned.1.call-update) | async-done | bytes 1572880 | tf_op jit(solution)/shard_map/all_gather | solution.py:46
  918.5 138.8 %all-gather.6.cloned.1.call-done = bf16[2,1,64,6144]{3,0,1,2:T(2,128)(2,1)} async-done(((bf16[2,1,1,6144]{3,0,1,2:T(2,128)(2,1)}), bf16[2,1,64,6144]{3,0,1,2:T(2,128)(2,1)}) %all-gather.6.cloned.1.call-update) | async-done | bytes 1572880 | tf_op jit(solution)/shard_map/all_gather | solution.py:53
  1057.4 3.2 fusion.10
  (10 shorter events, 0.0 us)
Async XLA Ops:
  7.2 0.8 copy-start.5
  7.2 0.8 copy-start.4
  7.2 32.4 %copy-start = (bf16[1,1,64,512]{3,2,1,0:T(8,128)(2,1)S(1)}, bf16[1,1,64,512]{3,2,1,0:T(8,128)(2,1)}, u32[]{:S(2)}) copy-start(bf16[1,1,64,512]{3,2,1,0:T(8,128)(2,1)} %param.9) | copy-start | bytes 196612
  7.2 32.4 %all-gather.4.cloned.1.call-start = ((), (), s32[]{:S(2)}) async-start(), calls=%async_computation | async-start | bytes 9437184 | tf_op jit(solution)/shard_map/all_gather | solution.py:44
  7.9 892.3 %all-reduce.3.cloned.1.call-start = ((), (), s32[]{:S(2)}) async-start(), calls=%async_computation.3 | async-start | bytes 6291456
  47.5 852.7 %copy-start.1 = (f32[2,1,1,6144]{3,2,1,0:T(1,128)S(1)}, f32[2,1,1,6144]{3,2,1,0:T(1,128)}, u32[]{:S(2)}) copy-start(f32[2,1,1,6144]{3,2,1,0:T(1,128)} %param.12) | copy-start | bytes 147460
  47.5 852.7 %copy-start.2 = (f32[2,1,1,6144]{3,2,1,0:T(1,128)S(1)}, f32[2,1,1,6144]{3,2,1,0:T(1,128)}, u32[]{:S(2)}) copy-start(f32[2,1,1,6144]{3,2,1,0:T(1,128)} %param.13) | copy-start | bytes 147460
  47.5 852.7 %copy-start.3 = (f32[2,1,1,6144]{3,2,1,0:T(1,128)S(1)}, f32[2,1,1,6144]{3,2,1,0:T(1,128)}, u32[]{:S(2)}) copy-start(f32[2,1,1,6144]{3,2,1,0:T(1,128)} %param.14) | copy-start | bytes 147460
  47.5 871.0 %all-gather.8.cloned.1.call-start = ((), (), s32[]{:S(2)}) async-start(), calls=%async_computation.2 | async-start | bytes 2359296 | tf_op jit(solution)/shard_map/all_gather | solution.py:46
  48.3 1009.1 %all-gather.6.cloned.1.call-start = ((), (), s32[]{:S(2)}) async-start(), calls=%async_computation.1 | async-start | bytes 1597440 | tf_op jit(solution)/shard_map/all_gather | solution.py:53
Sparse Core Ops, SparseCore 0:
  10.1 29.4 all-gather.3
  47.7 852.5 all-reduce.2
  902.5 15.9 all-gather.7
  924.3 132.9 all-gather.5
where the time goes:
time: 1070 us
  waiting for transfers between devices  1040 us (97%)
  between operations  13.8 us (1%)
    unnamed x5, waiting for transfers between devices  852 us
    all_gather x1, waiting for transfers between devices, per_device(): lax.all_gather(weights, 'dp', axis=2, tiled=True)  139 us
    all_gather x1, waiting for transfers between devices, per_device(): lax.all_gather(saved_rows, 'tensor', axis=3, tiled=True)[0, 0]  31.5 us
  transfers between devices with their start and end apart: 4, of which 4 were waited for; matrix products, arithmetic and copies ran while one was open for 1% of the time, Pallas kernels for 0%

commit v1 on v0

v1 whole, which is shorter than its diff:
```python
import jax
import jax.numpy as jnp
from jax import lax
from jax.experimental import pallas as pl
from jax.experimental.pallas import tpu as pltpu
from jax.sharding import Mesh
from jax.sharding import PartitionSpec as P

first_decay = 0.9
second_decay = 0.95
first_fix = 1.0 - 0.9**11
second_fix = 1.0 - 0.95**11
learn_rate = 0.01
weight_decay = 0.1
adam_epsilon = 1e-08

DP = ("x", "h", "z1", "z0")
NEAR = ("x", "z0")
FAR = ("tensor", "h", "z1")
LANES = 128
COLS = 24
BLOCK = 512

VMEM = pl.BlockSpec(memory_space=pltpu.VMEM)
SMEM = pl.BlockSpec(memory_space=pltpu.SMEM)
PARAMS = pltpu.CompilerParams(vmem_limit_bytes=16 * 1024 * 1024)


def adamw(grad, weight, first, second):
    new_first = first_decay * first + (1.0 - first_decay) * grad
    new_second = second_decay * second + (1.0 - second_decay) * grad * grad
    update = (
        new_first / first_fix / (jnp.sqrt(new_second / second_fix) + adam_epsilon)
        + weight_decay * weight
    )
    return (weight - learn_rate * update, new_first, new_second)


def grad_kernel(starts, sizes, hidden, rows, out):
    i = lax.broadcasted_iota(jnp.int32, (256, 128), 0)
    c = lax.broadcasted_iota(jnp.int32, (256, 128), 1)
    z1, h, t, z0, x = (i >> 1) & 3, (i >> 3) & 1, (i >> 4) & 1, (i >> 5) & 1, i >> 6
    source = t * 64 + x * 16 + h * 8 + z1 * 2 + z0
    pick = jnp.where(c == source, 1.0, 0.0).astype(jnp.bfloat16)
    spread = jnp.dot(pick, hidden[...].reshape(128, 512), preferred_element_type=jnp.float32)
    odd = (lax.broadcasted_iota(jnp.int32, (256, 512), 0) & 1) == 1
    line = lax.broadcasted_iota(jnp.int32, (256, 512), 1)
    low = jnp.where(odd, starts[0, 1], starts[0, 0])
    high = low + jnp.where(odd, sizes[0, 1], sizes[0, 0])
    masked = jnp.where((line >= low) & (line < high), spread, 0.0).astype(jnp.bfloat16)
    for k in range(3072 // BLOCK):
        piece = jnp.dot(
            masked, rows[:, k * BLOCK : (k + 1) * BLOCK], preferred_element_type=jnp.float32
        ).astype(jnp.bfloat16)
        for j in range(BLOCK // LANES):
            out[:, k * (BLOCK // LANES) + j] = piece[:, j * LANES : (j + 1) * LANES].reshape(
                8, 32, LANES
            )


def near_sum_kernel(parts, out, total):
    for j in range(COLS):
        total[j * 32 : (j + 1) * 32] = jnp.sum(parts[:, j].astype(jnp.float32), axis=0)
    for d in range(16):
        pair = [total[pl.ds(2 * d + e, COLS, stride=32), :] for e in range(2)]
        out[d] = jnp.concatenate(pair, axis=0).astype(jnp.bfloat16)


def step_kernel(parts, master, first, second, new_master, new_first, new_second, send):
    for t in range(2):
        grad = jnp.sum(parts[t * 8 : (t + 1) * 8].astype(jnp.float32), axis=0)
        weights = []
        for e in range(2):
            at = (e, pl.ds(t * COLS, COLS), slice(None))
            results = adamw(grad[e * COLS : (e + 1) * COLS], master[at], first[at], second[at])
            new_master[at], new_first[at], new_second[at] = results
            weights.append(results[0])
        both = jnp.concatenate(weights, axis=0).astype(jnp.bfloat16)
        for d in range(8):
            send[t * 8 + d] = both


def turn_kernel(got, out, wide):
    for r in range(16):
        wide[r * 48 : (r + 1) * 48] = got[r].astype(jnp.float32)
    for k in range(48):
        block = wide[pl.ds(k, 16, stride=48), :].astype(jnp.bfloat16)
        for d in range(8):
            out[d, k] = block


def gate_kernel(weights, inputs, out):
    for e in range(2):
        total = jnp.zeros((128, 64), jnp.float32)
        for j in range(0, COLS, 2):
            left = jnp.concatenate(
                [weights[:, e * COLS + j + i].reshape(128, LANES) for i in range(2)], axis=1
            )
            total += lax.dot_general(
                left,
                inputs[e, :, j * LANES : (j + 2) * LANES],
                (((1,), (1,)), ((), ())),
                preferred_element_type=jnp.float32,
            )
        for x in range(4):
            for z0 in range(2):
                for t in range(2):
                    row = (x * 2 + z0) * 16 + t * 8
                    out[t, e, pl.ds(x * 16 + z0, 8, stride=2), :] = total[row : row + 8]


def call(kernel, out_shape, in_specs, scratch=()):
    many = isinstance(out_shape, (list, tuple))
    return pl.pallas_call(
        kernel,
        out_shape=out_shape,
        in_specs=in_specs,
        out_specs=[VMEM] * len(out_shape) if many else VMEM,
        scratch_shapes=list(scratch),
        compiler_params=PARAMS,
    )


def swap(array, axes):
    return lax.all_to_all(array, axes, 0, 0, tiled=True)


def per_device(saved_rows, grad_hidden, counts, offsets, master, moment1, moment2, next_rows):
    bf16, f32 = jnp.bfloat16, jnp.float32
    shape = jax.ShapeDtypeStruct
    hidden = swap(jnp.broadcast_to(grad_hidden[0, 0], (2, 64, 512)), "tensor")
    parts = call(grad_kernel, shape((8, COLS, 32, LANES), bf16), [SMEM, SMEM, VMEM, VMEM])(
        offsets, counts, hidden, saved_rows[0, 0]
    )
    parts = swap(parts, NEAR)
    parts = call(
        near_sum_kernel, shape((16, 48, LANES), bf16), [VMEM], [pltpu.VMEM((COLS * 32, LANES), f32)]
    )(parts)
    parts = swap(parts, FAR)
    state = [a.reshape(2, 48, LANES) for a in (master, moment1, moment2)]
    *new, send = call(
        step_kernel, [shape((2, 48, LANES), f32)] * 3 + [shape((16, 48, LANES), bf16)], [VMEM] * 4
    )(parts, *state)
    got = swap(send, FAR)
    got = call(
        turn_kernel, shape((8, 48, 16, LANES), bf16), [VMEM], [pltpu.VMEM((16 * 48, LANES), f32)]
    )(got)
    got = swap(got, NEAR)
    gates = call(gate_kernel, shape((2, 2, 64, 64), f32), [VMEM, VMEM])(got, next_rows[0])
    gates = swap(gates, "tensor")
    scale = 6144 ** (-0.5)
    next_gate = (gates[0] + gates[1]) * scale
    return (*[a.reshape(2, 1, 1, 6144) for a in new], next_gate[None])


def solution(mesh):
    fine = Mesh(
        mesh.devices.reshape(4, 2, 4, 2, 4, 2), ("x", "h", "z1", "z0", "expert", "tensor")
    )
    shard = P("expert", "tensor", DP, None)
    placed = (
        P(DP, "expert", None, "tensor"),
        P(DP, "expert", "tensor", None),
        P(DP, "expert"),
        P(DP, "expert"),
        shard,
        shard,
        shard,
        P(DP, "expert", None, "tensor"),
    )
    return jax.shard_map(
        per_device,
        mesh=fine,
        in_specs=placed,
        out_specs=(shard, shard, shard, P(DP, "expert", "tensor", None)),
        check_vma=False,
    )
```

time: 1070 us -> 118 us (0.11)
  waiting for transfers between devices: 1040 us -> 0 us
  blocking collectives: 0 us -> 107 us
  between operations: 13.8 us -> 0.69 us
    unnamed x5 -> x0, waiting for transfers between devices: 852 us -> none
    all_gather x3 -> x0, waiting for transfers between devices: 184 us -> none  [the longest x1 139 us: per_device(): lax.all_gather(weights, 'dp', axis=2, tiled=True)]
    all_to_all x0 -> x6, blocking collectives: none -> 107 us  [swap(): return lax.all_to_all(array, axes, 0, 0, tiled=True)]
  transfers between devices with their start and end apart: 4 -> 0, of which waited for: 4 -> 0; matrix products, arithmetic and copies ran while one was open for 1% -> 0% of each run, Pallas kernels for 0% -> 0%
where the time goes in v1:
time: 118 us
  blocking collectives  107 us (91%)
  local copies, waits for them, and re-layouts  4.84 us (4%)
  Pallas kernels  3.54 us (3%)
  other arithmetic  1.48 us (1%)
    all_to_all x6, blocking collectives, swap(): return lax.all_to_all(array, axes, 0, 0, tiled=True)  107 us
    unnamed x16, local copies, waits for them, and re-layouts  3.48 us

profile of v1, /device:TPU:8, one launch (start us, length us, event | category | flops | bytes accessed | tf_op | source)
XLA Modules:
  0.0 117.7 jit_solution(12302332892715260424)
XLA Ops:
  0.6 0.8 broadcast_in_dim.4
  1.5 3.8 %all_to_all.30.hidden = bf16[2,64,512]{2,1,0:T(8,128)(2,1)S(1)} all-to-all(bf16[2,64,512]{2,1,0:T(8,128)(2,1)S(1)} %broadcast_in_dim.4), channel_id=1, replica_groups=mesh['x'=4,'h'=2,'z1'=4,'z0'=2,'expert'=4,'tensor'=2] {'tensor'}, dimensions={0} | all-to-all | bytes 262144 | tf_op jit(solution)/shard_map/all_to_all | solution.py:125
  5.3 1.9 %copy-done = bf16[1,1,512,3072]{3,2,1,0:T(8,128)(2,1)S(1)} copy-done((bf16[1,1,512,3072]{3,2,1,0:T(8,128)(2,1)S(1)}, bf16[1,1,512,3072]{3,2,1,0:T(8,128)(2,1)}, u32[]{:S(2)}) %copy-start) | copy-done | bytes 3145752
  7.2 0.7 copy-done.5
  7.9 0.7 copy-done.6
  8.5 1.7 %shard_map.111 = bf16[8,24,32,128]{3,2,1,0:T(8,128)(2,1)S(1)} custom-call(s32[1,2]{1,0:T(1,128)S(1)} %copy-done.5, s32[1,2]{1,0:T(1,128)S(1)} %copy-done.6, bf16[2,64,512]{2,1,0:T(8,128)(2,1)S(1)} %all_to_all.30.hidden, bf16[512,3072]{1,0:T(8,128)(2,1)S(1)} %bitcast.9), custom_call_target="tpu_custom_call" | custom-call | tf_op jit(solution)/shard_map/pallas_call | solution.py:132
  10.2 27.5 %all_to_all.31.parts = bf16[8,24,32,128]{3,2,1,0:T(8,128)(2,1)S(1)} all-to-all(bf16[8,24,32,128]{3,2,1,0:T(8,128)(2,1)S(1)} %shard_map.111), channel_id=1, replica_groups=mesh['x'=4,'h'=2,'z1'=4,'z0'=2,'expert'=4,'tensor'=2] {'x','z0'}, dimensions={0} | all-to-all | bytes 3145728 | tf_op jit(solution)/shard_map/all_to_all | solution.py:125
  37.8 0.4 shard_map.112
  38.2 29.7 %all_to_all.32.parts = bf16[16,48,128]{2,1,0:T(8,128)(2,1)S(1)} all-to-all(bf16[16,48,128]{2,1,0:T(8,128)(2,1)S(1)} %shard_map.112), channel_id=1, replica_groups=mesh['x'=4,'h'=2,'z1'=4,'z0'=2,'expert'=4,'tensor'=2] {'tensor','h','z1'}, dimensions={0} | all-to-all | bytes 393216 | tf_op jit(solution)/shard_map/all_to_all | solution.py:125
  67.9 0.0 copy-done.2
  67.9 0.0 copy-done.3
  67.9 0.0 copy-done.4
  67.9 0.7 shard_map.113
  68.6 18.1 %all_to_all.33.got = bf16[16,48,128]{2,1,0:T(8,128)(2,1)S(1)} all-to-all(bf16[16,48,128]{2,1,0:T(8,128)(2,1)S(1)} %get-tuple-element.11), channel_id=1, replica_groups=mesh['x'=4,'h'=2,'z1'=4,'z0'=2,'expert'=4,'tensor'=2] {'tensor','h','z1'}, dimensions={0} | all-to-all | bytes 393216 | tf_op jit(solution)/shard_map/all_to_all | solution.py:125
  86.7 0.2 shard_map.114
  86.9 0.0 copy-start.1
  86.9 24.2 %all_to_all.34.weights = bf16[8,48,16,128]{3,2,1,0:T(8,128)(2,1)S(1)} all-to-all(bf16[8,48,16,128]{3,2,1,0:T(8,128)(2,1)S(1)} %shard_map.114), channel_id=1, replica_groups=mesh['x'=4,'h'=2,'z1'=4,'z0'=2,'expert'=4,'tensor'=2] {'x','z0'}, dimensions={0} | all-to-all | bytes 3145728 | tf_op jit(solution)/shard_map/all_to_all | solution.py:125
  111.1 0.5 shard_map.115
  111.7 0.1 reshape.32
  111.8 3.8 %all_to_all.35 = f32[2,1,8192]{2,1,0:T(1,128)S(1)} all-to-all(f32[2,1,8192]{2,1,0:T(1,128)S(1)} %reshape.32), channel_id=1, replica_groups=mesh['x'=4,'h'=2,'z1'=4,'z0'=2,'expert'=4,'tensor'=2] {'tensor'}, dimensions={0} | all-to-all | bytes 131072 | tf_op jit(solution)/shard_map/all_to_all | solution.py:125
  115.6 0.5 broadcast.1
  116.1 0.8 reduce
  116.9 0.1 reshape.33
  117.1 0.6 fusion
  (7 shorter events, 0.0 us)
Async XLA Ops:
  5.3 1.9 %copy-start = (bf16[1,1,512,3072]{3,2,1,0:T(8,128)(2,1)S(1)}, bf16[1,1,512,3072]{3,2,1,0:T(8,128)(2,1)}, u32[]{:S(2)}) copy-start(bf16[1,1,512,3072]{3,2,1,0:T(8,128)(2,1)} %param.8) | copy-start | bytes 9437188
  7.2 0.7 copy-start.5
  7.9 0.7 copy-start.6
  37.8 30.1 %copy-start.2 = (f32[2,1,1,6144]{3,2,1,0:T(1,128)S(1)}, f32[2,1,1,6144]{3,2,1,0:T(1,128)}, u32[]{:S(2)}) copy-start(f32[2,1,1,6144]{3,2,1,0:T(1,128)} %param.12) | copy-start | bytes 147460
  37.8 30.1 %copy-start.3 = (f32[2,1,1,6144]{3,2,1,0:T(1,128)S(1)}, f32[2,1,1,6144]{3,2,1,0:T(1,128)}, u32[]{:S(2)}) copy-start(f32[2,1,1,6144]{3,2,1,0:T(1,128)} %param.13) | copy-start | bytes 147460
  37.8 30.1 %copy-start.4 = (f32[2,1,1,6144]{3,2,1,0:T(1,128)S(1)}, f32[2,1,1,6144]{3,2,1,0:T(1,128)}, u32[]{:S(2)}) copy-start(f32[2,1,1,6144]{3,2,1,0:T(1,128)} %param.14) | copy-start | bytes 147460
  86.9 24.2 %copy-start.1 = (bf16[1,2,64,3072]{3,2,1,0:T(8,128)(2,1)S(1)}, bf16[1,2,64,3072]{3,2,1,0:T(8,128)(2,1)}, u32[]{:S(2)}) copy-start(bf16[1,2,64,3072]{3,2,1,0:T(8,128)(2,1)} %param.15) | copy-start | bytes 2359300

commit v2 on v1

v2 whole, which is shorter than its diff:
```python
import jax
import jax.numpy as jnp
from jax import lax
from jax.experimental import pallas as pl
from jax.experimental.pallas import tpu as pltpu
from jax.sharding import Mesh
from jax.sharding import PartitionSpec as P

first_decay = 0.9
second_decay = 0.95
first_fix = 1.0 - 0.9**11
second_fix = 1.0 - 0.95**11
learn_rate = 0.01
weight_decay = 0.1
adam_epsilon = 1e-08

DP = ("x", "h", "z1", "z0")
NEAR = ("x", "z0")
FAR = ("tensor", "h", "z1")
LANES = 128
COLS = 24
BLOCK = 512
PIECES = 3072 // BLOCK
GROUP = BLOCK // LANES

VMEM = pl.BlockSpec(memory_space=pltpu.VMEM)
HBM = pl.BlockSpec(memory_space=pltpu.HBM)


def adamw(grad, weight, first, second):
    new_first = first_decay * first + (1.0 - first_decay) * grad
    new_second = second_decay * second + (1.0 - second_decay) * grad * grad
    update = (
        new_first / first_fix / (jnp.sqrt(new_second / second_fix) + adam_epsilon)
        + weight_decay * weight
    )
    return (weight - learn_rate * update, new_first, new_second)


def stage_kernel(starts, sizes, mine, rows, held, hidden, inside, start_at, size_of, sems):
    small = [
        pltpu.make_async_copy(starts, start_at, sems.at[0]),
        pltpu.make_async_copy(sizes, size_of, sems.at[1]),
    ]
    large = [
        pltpu.make_async_copy(mine, hidden, sems.at[2]),
        pltpu.make_async_copy(rows, held, sems.at[3]),
    ]
    for copy in small + large:
        copy.start()
    for copy in small:
        copy.wait()
    odd = (lax.broadcasted_iota(jnp.int32, (256, 512), 0) & 1) == 1
    line = lax.broadcasted_iota(jnp.int32, (256, 512), 1)
    low = jnp.where(odd, start_at[0, 1], start_at[0, 0])
    high = low + jnp.where(odd, size_of[0, 1], size_of[0, 0])
    inside[...] = jnp.where((line >= low) & (line < high), 1.0, 0.0).astype(jnp.bfloat16)
    for copy in large:
        copy.wait()


def grad_kernel(mine, other, inside, rows, out, ready, sems):
    stores = [
        pltpu.make_async_copy(ready.at[k], out.at[:, pl.ds(k * GROUP, GROUP)], sems.at[k])
        for k in range(PIECES)
    ]
    me = lax.axis_index("tensor")
    i = lax.broadcasted_iota(jnp.int32, (256, 64), 0)
    c = lax.broadcasted_iota(jnp.int32, (256, 64), 1)
    z1, h, t, z0, x = (i >> 1) & 3, (i >> 3) & 1, (i >> 4) & 1, (i >> 5) & 1, i >> 6
    found = c == x * 16 + h * 8 + z1 * 2 + z0
    picks = [jnp.where(found & (t == w), 1.0, 0.0).astype(jnp.bfloat16) for w in (me, 1 - me)]
    spread = jnp.dot(picks[0], mine[...], preferred_element_type=jnp.float32)
    spread += jnp.dot(picks[1], other[...], preferred_element_type=jnp.float32)
    masked = jnp.where(inside[...] != 0, spread.astype(jnp.bfloat16), 0)
    for k in range(PIECES):
        piece = jnp.dot(
            masked, rows[:, k * BLOCK : (k + 1) * BLOCK], preferred_element_type=jnp.float32
        ).astype(jnp.bfloat16)
        for j in range(GROUP):
            ready[k, :, j] = piece[:, j * LANES : (j + 1) * LANES].reshape(8, 32, LANES)
        stores[k].start()
    for copy in stores:
        copy.wait()


def near_sum_kernel(parts, unused, out, total):
    del unused
    for j in range(COLS):
        total[j * 32 : (j + 1) * 32] = jnp.sum(parts[:, j].astype(jnp.float32), axis=0)
    for d in range(16):
        pair = [total[pl.ds(2 * d + e, COLS, stride=32), :] for e in range(2)]
        out[d] = jnp.concatenate(pair, axis=0).astype(jnp.bfloat16)


def step_kernel(parts, master, first, second, new_master, new_first, new_second, send):
    weights = [[None, None], [None, None]]
    for t in range(2):
        grad = jnp.sum(parts[t * 8 : (t + 1) * 8].astype(jnp.float32), axis=0)
        for e in range(2):
            at = (e, pl.ds(t * COLS, COLS), slice(None))
            results = adamw(grad[e * COLS : (e + 1) * COLS], master[at], first[at], second[at])
            new_master[at], new_first[at], new_second[at] = results
            weights[e][t] = results[0]
    block = jnp.concatenate(weights[0] + weights[1], axis=0).astype(jnp.bfloat16)
    for d in range(8):
        send[d] = block


def turn_kernel(got, out, wide):
    for r in range(8):
        wide[r * 96 : (r + 1) * 96] = got[r].astype(jnp.float32)
    for k in range(48):
        pair = [wide[pl.ds(e * 48 + k, 8, stride=96), :] for e in range(2)]
        block = jnp.concatenate(pair, axis=0).astype(jnp.bfloat16)
        for d in range(8):
            out[d, k] = block


def gate_kernel(weights, near, far, out):
    me = lax.axis_index("tensor")
    total = jnp.zeros((128, 128), jnp.float32)
    for inputs, half in ((near, me), (far, 1 - me)):
        for j in range(0, COLS, 2):
            left = [weights[:, half * COLS + j + i].reshape(128, LANES) for i in range(2)]
            right = inputs[:, :, j * LANES : (j + 2) * LANES].reshape(128, 2 * LANES)
            total += lax.dot_general(
                jnp.concatenate(left, axis=1),
                right,
                (((1,), (1,)), ((), ())),
                preferred_element_type=jnp.float32,
            )
    total = total * (6144 ** (-0.5))
    for e in range(2):
        own = total[:, e * 64 : (e + 1) * 64]
        for x in range(4):
            for z0 in range(2):
                row = (x * 2 + z0) * 16 + e * 8
                out[e, pl.ds(x * 16 + z0, 8, stride=2), :] = own[row : row + 8]


def call(kernel, out_shape, in_specs, scratch=(), out_specs=None):
    many = isinstance(out_shape, (list, tuple))
    return pl.pallas_call(
        kernel,
        out_shape=out_shape,
        in_specs=in_specs,
        out_specs=out_specs or ([VMEM] * len(out_shape) if many else VMEM),
        scratch_shapes=list(scratch),
        compiler_params=pltpu.CompilerParams(vmem_limit_bytes=16 << 20),
    )


def swap(array, axes):
    return lax.all_to_all(array, axes, 0, 0, tiled=True)


def per_device(saved_rows, grad_hidden, counts, offsets, master, moment1, moment2, next_rows):
    bf16, f32 = jnp.bfloat16, jnp.float32
    shape = jax.ShapeDtypeStruct
    mine = grad_hidden[0, 0]
    other = lax.ppermute(mine, "tensor", [(0, 1), (1, 0)])
    far_inputs = lax.ppermute(next_rows[0], "tensor", [(0, 1), (1, 0)])
    held, hidden, inside = call(
        stage_kernel,
        [
            pltpu.VMEM((512, 3072), bf16),
            pltpu.VMEM((64, 512), bf16),
            pltpu.VMEM((256, 512), bf16),
        ],
        [HBM] * 4,
        [pltpu.SMEM((1, 2), jnp.int32)] * 2 + [pltpu.SemaphoreType.DMA((4,))],
    )(
        *[
            pltpu.with_memory_space_constraint(a, pltpu.HBM)
            for a in (offsets, counts, mine, saved_rows[0, 0])
        ]
    )
    parts = call(
        grad_kernel,
        pltpu.HBM((8, COLS, 32, LANES), bf16),
        [VMEM] * 4,
        [
            pltpu.VMEM((PIECES, 8, GROUP, 32, LANES), bf16),
            pltpu.SemaphoreType.DMA((PIECES,)),
        ],
        out_specs=HBM,
    )(hidden, other, inside, held)
    parts = swap(parts, NEAR)
    parts = call(
        near_sum_kernel,
        shape((16, 48, LANES), bf16),
        [VMEM, HBM],
        [pltpu.VMEM((COLS * 32, LANES), f32)],
    )(parts, far_inputs)
    parts = swap(parts, FAR)
    state = [a.reshape(2, 48, LANES) for a in (master, moment1, moment2)]
    *new, send = call(
        step_kernel, [shape((2, 48, LANES), f32)] * 3 + [shape((8, 96, LANES), bf16)], [VMEM] * 4
    )(parts, *state)
    got = swap(send, ("h", "z1"))
    got = call(
        turn_kernel, shape((8, 48, 16, LANES), bf16), [VMEM], [pltpu.VMEM((8 * 96, LANES), f32)]
    )(got)
    got = swap(got, NEAR)
    gates = call(gate_kernel, shape((2, 64, 64), f32), [VMEM] * 3)(
        got, next_rows[0], far_inputs
    )
    return (*[a.reshape(2, 1, 1, 6144) for a in new], gates[None])


def solution(mesh):
    fine = Mesh(
        mesh.devices.reshape(4, 2, 4, 2, 4, 2), ("x", "h", "z1", "z0", "expert", "tensor")
    )
    shard = P("expert", "tensor", DP, None)
    placed = (
        P(DP, "expert", None, "tensor"),
        P(DP, "expert", "tensor", None),
        P(DP, "expert"),
        P(DP, "expert"),
        shard,
        shard,
        shard,
        P(DP, "expert", None, "tensor"),
    )
    return jax.shard_map(
        per_device,
        mesh=fine,
        in_specs=placed,
        out_specs=(shard, shard, shard, P(DP, "expert", "tensor", None)),
        check_vma=False,
    )
```

time: 118 us -> 108 us (0.915)
  blocking collectives: 107 us -> 70.1 us
  waiting for transfers between devices: 0 us -> 19.7 us
  starting transfers between devices: 0 us -> 10.4 us
  local copies, waits for them, and re-layouts: 4.84 us -> 0.02 us
  Pallas kernels: 3.54 us -> 6.57 us
  other arithmetic: 1.48 us -> 0 us
    all_to_all x6 -> x3, blocking collectives: 107 us -> 70.1 us  [swap(): return lax.all_to_all(array, axes, 0, 0, tiled=True)]
    all_to_all x0 -> x1, waiting for transfers between devices: none -> 17.7 us  [swap(): return lax.all_to_all(array, axes, 0, 0, tiled=True)]
    all_to_all x0 -> x1, starting transfers between devices: none -> 6.25 us  [swap(): return lax.all_to_all(array, axes, 0, 0, tiled=True)]
    ppermute x0 -> x2, starting transfers between devices: none -> 4.18 us  [the longest x1 2.26 us: per_device(): far_inputs = lax.ppermute(next_rows[0], 'tensor', [(0, 1), (1, 0)])]
    unnamed x16 -> x8, local copies, waits for them, and re-layouts: 3.48 us -> 0.02 us
    pallas_call x5 -> x6, Pallas kernels: 3.54 us -> 6.57 us  [the longest x1 1.97 us: per_device(): call(stage_kernel, [pltpu.VMEM((512, 3072), bf16), pltpu.VMEM((64, 512),...]
    ppermute x0 -> x2, waiting for transfers between devices: none -> 2.05 us  [the longest x1 2.05 us: per_device(): far_inputs = lax.ppermute(next_rows[0], 'tensor', [(0, 1), (1, 0)])]
  transfers between devices with their start and end apart: 0 -> 3, of which waited for: 0 -> 2; matrix products, arithmetic and copies ran while one was open for 0% -> 0% of each run, Pallas kernels for 0% -> 2%
where the time goes in v2:
time: 108 us
  blocking collectives  70.1 us (65%)
  waiting for transfers between devices  19.7 us (18%)
  starting transfers between devices  10.4 us (10%)
  Pallas kernels  6.57 us (6%)
    all_to_all x3, blocking collectives, swap(): return lax.all_to_all(array, axes, 0, 0, tiled=True)  70.1 us
    all_to_all x1, waiting for transfers between devices, swap(): return lax.all_to_all(array, axes, 0, 0, tiled=True)  17.7 us
    all_to_all x1, starting transfers between devices, swap(): return lax.all_to_all(array, axes, 0, 0, tiled=True)  6.25 us
    ppermute x1, starting transfers between devices, per_device(): far_inputs = lax.ppermute(next_rows[0], 'tensor', [(0, 1), (1, 0)])  2.26 us
  transfers between devices with their start and end apart: 3, of which 2 were waited for; matrix products, arithmetic and copies ran while one was open for 0% of the time, Pallas kernels for 2%

profile of v2, /device:TPU:8, one launch (start us, length us, event | category | flops | bytes accessed | tf_op | source)
XLA Modules:
  0.0 107.6 jit_solution(858242643684991859)
XLA Ops:
  0.6 1.9 %collective-permute-start = (bf16[64,512]{1,0:T(8,128)(2,1)}, bf16[64,512]{1,0:T(8,128)(2,1)S(1)}, u32[]{:S(2)}, u32[]{:S(2)}) collective-permute-start(bf16[64,512]{1,0:T(8,128)(2,1)} %bitcast.16), channel_id=1, source_target_pairs={{0,1},{1,0},{2,3},{3,2},{4,5},{5,4},{6,7},{7,6},{8,9},{9,8},{10,11... | collective-permute-start | bytes 196616 | tf_op jit(solution)/shard_map/ppermute | solution.py:162
  2.6 2.0 %shard_map.111 = (bf16[512,3072]{1,0:T(8,128)(2,1)S(1)}, bf16[64,512]{1,0:T(8,128)(2,1)S(1)}, bf16[256,512]{1,0:T(8,128)(2,1)S(1)}) custom-call(s32[1,2]{1,0:T(1,128)} %starts.1, s32[1,2]{1,0:T(1,128)} %sizes.1, bf16[64,512]{1,0:T(8,128)(2,1)} %bitcast.17, bf16[512,3072]{1,0:T(8,128)(2,1)} %bitcast.15), custom_call_target="tpu_custom_call" | custom-call | tf_op jit(solution)/shard_map/pallas_call | solution.py:164
  4.5 0.0 collective-permute-done.other
  4.5 1.9 %shard_map.112 = bf16[8,24,32,128]{3,2,1,0:T(8,128)(2,1)} custom-call(bf16[64,512]{1,0:T(8,128)(2,1)S(1)} %get-tuple-element.11.mine, bf16[64,512]{1,0:T(8,128)(2,1)S(1)} %collective-permute-done.other, bf16[256,512]{1,0:T(8,128)(2,1)S(1)} %get-tuple-element.12.inside, bf16[512,3072]{1,0:T(8,128)(2,1)S(1)} %get-tuple-element.13.rows), custom_call_target="tpu_custom_call" | custom-call | tf_op jit(solution)/shard_map/pallas_call | solution.py:179
  6.5 0.0 copy-start
  6.5 6.3 %all-to-all-start = ((bf16[8,24,32,128]{3,2,1,0:T(8,128)(2,1)}), bf16[8,24,32,128]{3,2,1,0:T(8,128)(2,1)S(1)}, u32[]{:S(2)}, u32[]{:S(2)}) async-start(bf16[8,24,32,128]{3,2,1,0:T(8,128)(2,1)} %shard_map.112), calls=%async_computation | async-start | bytes 3145728 | tf_op jit(solution)/shard_map/all_to_all | solution.py:155
  12.8 0.0 copy-start.1
  12.8 0.0 copy-start.2
  12.8 0.0 copy-start.3
  12.8 0.0 copy-done
  12.8 2.3 %collective-permute-start.1 = (bf16[2,64,3072]{2,1,0:T(8,128)(2,1)S(1)}, bf16[2,64,3072]{2,1,0:T(8,128)(2,1)S(1)}, u32[]{:S(2)}, u32[]{:S(2)}) collective-permute-start(bf16[2,64,3072]{2,1,0:T(8,128)(2,1)S(1)} %bitcast.10), channel_id=1, source_target_pairs={{0,1},{1,0},{2,3},{3,2},{4,5},{5,4},{6,7},{7,6},{8,9},{9,8},{10,11... | collective-permute-start | bytes 2359304 | tf_op jit(solution)/shard_map/ppermute | solution.py:163
  15.1 2.0 %collective-permute-done.1.unused.far = bf16[2,64,3072]{2,1,0:T(8,128)(2,1)S(1)} collective-permute-done((bf16[2,64,3072]{2,1,0:T(8,128)(2,1)S(1)}, bf16[2,64,3072]{2,1,0:T(8,128)(2,1)S(1)}, u32[]{:S(2)}, u32[]{:S(2)}) %collective-permute-start.1) | collective-permute-done | bytes 786464 | tf_op jit(solution)/shard_map/ppermute | solution.py:163
  17.1 17.7 %all-to-all-done.parts = bf16[8,24,32,128]{3,2,1,0:T(8,128)(2,1)S(1)} async-done(((bf16[8,24,32,128]{3,2,1,0:T(8,128)(2,1)}), bf16[8,24,32,128]{3,2,1,0:T(8,128)(2,1)S(1)}, u32[]{:S(2)}, u32[]{:S(2)}) %all-to-all-start) | async-done | bytes 1572896 | tf_op jit(solution)/shard_map/all_to_all | solution.py:155
  34.8 0.4 shard_map.113
  35.2 29.6 %all_to_all.20.parts = bf16[16,48,128]{2,1,0:T(8,128)(2,1)S(1)} all-to-all(bf16[16,48,128]{2,1,0:T(8,128)(2,1)S(1)} %shard_map.113), channel_id=1, replica_groups=mesh['x'=4,'h'=2,'z1'=4,'z0'=2,'expert'=4,'tensor'=2] {'tensor','h','z1'}, dimensions={0} | all-to-all | bytes 393216 | tf_op jit(solution)/shard_map/all_to_all | solution.py:155
  64.8 0.0 copy-done.1
  64.8 0.0 copy-done.2
  64.8 0.0 copy-done.3
  64.8 0.7 shard_map.114
  65.6 16.9 %all_to_all.21.got = bf16[8,96,128]{2,1,0:T(8,128)(2,1)S(1)} all-to-all(bf16[8,96,128]{2,1,0:T(8,128)(2,1)S(1)} %get-tuple-element.17), channel_id=1, replica_groups=mesh['x'=4,'h'=2,'z1'=4,'z0'=2,'expert'=4,'tensor'=2] {'h','z1'}, dimensions={0} | all-to-all | bytes 393216 | tf_op jit(solution)/shard_map/all_to_all | solution.py:155
  82.5 0.3 shard_map.115
  82.8 23.5 %all_to_all.22.weights = bf16[8,48,16,128]{3,2,1,0:T(8,128)(2,1)S(1)} all-to-all(bf16[8,48,16,128]{3,2,1,0:T(8,128)(2,1)S(1)} %shard_map.115), channel_id=1, replica_groups=mesh['x'=4,'h'=2,'z1'=4,'z0'=2,'expert'=4,'tensor'=2] {'x','z0'}, dimensions={0} | all-to-all | bytes 3145728 | tf_op jit(solution)/shard_map/all_to_all | solution.py:155
  106.3 1.3 %shard_map.116 = f32[2,64,64]{2,1,0:T(8,128)} custom-call(bf16[8,48,16,128]{3,2,1,0:T(8,128)(2,1)S(1)} %all_to_all.22.weights, bf16[2,64,3072]{2,1,0:T(8,128)(2,1)S(1)} %bitcast.11, bf16[2,64,3072]{2,1,0:T(8,128)(2,1)S(1)} %collective-permute-done.1.unused.far), custom_call_target="tpu_custom_call" | custom-call | tf_op jit(solution)/shard_map/pallas_call | solution.py:206
Async XLA Ops:
  0.6 3.9 %collective-permute-start = (bf16[64,512]{1,0:T(8,128)(2,1)}, bf16[64,512]{1,0:T(8,128)(2,1)S(1)}, u32[]{:S(2)}, u32[]{:S(2)}) collective-permute-start(bf16[64,512]{1,0:T(8,128)(2,1)} %bitcast.16), channel_id=1, source_target_pairs={{0,1},{1,0},{2,3},{3,2},{4,5},{5,4},{6,7},{7,6},{8,9},{9,8},{10,11... | collective-permute-start | bytes 196616 | tf_op jit(solution)/shard_map/ppermute | solution.py:162
  6.5 6.3 %copy-start = (bf16[1,2,64,3072]{3,2,1,0:T(8,128)(2,1)S(1)}, bf16[1,2,64,3072]{3,2,1,0:T(8,128)(2,1)}, u32[]{:S(2)}) copy-start(bf16[1,2,64,3072]{3,2,1,0:T(8,128)(2,1)} %param.15) | copy-start | bytes 2359300
  6.5 28.3 %all-to-all-start = ((bf16[8,24,32,128]{3,2,1,0:T(8,128)(2,1)}), bf16[8,24,32,128]{3,2,1,0:T(8,128)(2,1)S(1)}, u32[]{:S(2)}, u32[]{:S(2)}) async-start(bf16[8,24,32,128]{3,2,1,0:T(8,128)(2,1)} %shard_map.112), calls=%async_computation | async-start | bytes 3145728 | tf_op jit(solution)/shard_map/all_to_all | solution.py:155
  12.8 52.1 %copy-start.1 = (f32[2,1,1,6144]{3,2,1,0:T(1,128)S(1)}, f32[2,1,1,6144]{3,2,1,0:T(1,128)}, u32[]{:S(2)}) copy-start(f32[2,1,1,6144]{3,2,1,0:T(1,128)} %param.12) | copy-start | bytes 147460
  12.8 52.1 %copy-start.2 = (f32[2,1,1,6144]{3,2,1,0:T(1,128)S(1)}, f32[2,1,1,6144]{3,2,1,0:T(1,128)}, u32[]{:S(2)}) copy-start(f32[2,1,1,6144]{3,2,1,0:T(1,128)} %param.13) | copy-start | bytes 147460
  12.8 52.1 %copy-start.3 = (f32[2,1,1,6144]{3,2,1,0:T(1,128)S(1)}, f32[2,1,1,6144]{3,2,1,0:T(1,128)}, u32[]{:S(2)}) copy-start(f32[2,1,1,6144]{3,2,1,0:T(1,128)} %param.14) | copy-start | bytes 147460
  12.8 4.3 %collective-permute-start.1 = (bf16[2,64,3072]{2,1,0:T(8,128)(2,1)S(1)}, bf16[2,64,3072]{2,1,0:T(8,128)(2,1)S(1)}, u32[]{:S(2)}, u32[]{:S(2)}) collective-permute-start(bf16[2,64,3072]{2,1,0:T(8,128)(2,1)S(1)} %bitcast.10), channel_id=1, source_target_pairs={{0,1},{1,0},{2,3},{3,2},{4,5},{5,4},{6,7},{7,6},{8,9},{9,8},{10,11... | collective-permute-start | bytes 2359304 | tf_op jit(solution)/shard_map/ppermute | solution.py:163

commit v3 on v2

--- a/solution.py
+++ b/solution.py
@@ -84,8 +84,7 @@
         copy.wait()
 
 
-def near_sum_kernel(parts, unused, out, total):
-    del unused
+def near_sum_kernel(parts, out, total):
     for j in range(COLS):
         total[j * 32 : (j + 1) * 32] = jnp.sum(parts[:, j].astype(jnp.float32), axis=0)
     for d in range(16):
@@ -93,50 +92,61 @@
         out[d] = jnp.concatenate(pair, axis=0).astype(jnp.bfloat16)
 
 
-def step_kernel(parts, master, first, second, new_master, new_first, new_second, send):
-    weights = [[None, None], [None, None]]
+def step_kernel(parts, master, first, second, new_master, new_first, new_second, send, block, sems):
+    copies = [
+        pltpu.make_async_copy(
+            block.at[pl.ds(t * 16, 16)], send.at[pl.ds(t * 16, 16)], sems.at[t]
+        )
+        for t in range(2)
+    ]
     for t in range(2):
         grad = jnp.sum(parts[t * 8 : (t + 1) * 8].astype(jnp.float32), axis=0)
+        weights = []
         for e in range(2):
             at = (e, pl.ds(t * COLS, COLS), slice(None))
             results = adamw(grad[e * COLS : (e + 1) * COLS], master[at], first[at], second[at])
             new_master[at], new_first[at], new_second[at] = results
-            weights[e][t] = results[0]
-    block = jnp.concatenate(weights[0] + weights[1], axis=0).astype(jnp.bfloat16)
-    for d in range(8):
-        send[d] = block
-
-
-def turn_kernel(got, out, wide):
-    for r in range(8):
-        wide[r * 96 : (r + 1) * 96] = got[r].astype(jnp.float32)
-    for k in range(48):
-        pair = [wide[pl.ds(e * 48 + k, 8, stride=96), :] for e in range(2)]
-        block = jnp.concatenate(pair, axis=0).astype(jnp.bfloat16)
-        for d in range(8):
-            out[d, k] = block
-
-
-def gate_kernel(weights, near, far, out):
-    me = lax.axis_index("tensor")
-    total = jnp.zeros((128, 128), jnp.float32)
-    for inputs, half in ((near, me), (far, 1 - me)):
+            weights.append(results[0])
+        both = jnp.concatenate(weights, axis=0).astype(jnp.bfloat16)
+        for d in range(16):
+            block[t * 16 + d] = both
+        copies[t].start()
+    for copy in copies:
+        copy.wait()
+
+
+def gate_kernel(got, own, ahead, opposite, back, out, wide):
+    me = lax.axis_index("x")
+    step = 1 - 2 * lax.axis_index("tensor")
+    for r in range(32):
+        wide[r * 48 : (r + 1) * 48] = got[r].astype(jnp.float32)
+    totals = []
+    for e in range(2):
+        total = jnp.zeros((32, 256), jnp.float32)
         for j in range(0, COLS, 2):
-            left = [weights[:, half * COLS + j + i].reshape(128, LANES) for i in range(2)]
-            right = inputs[:, :, j * LANES : (j + 2) * LANES].reshape(128, 2 * LANES)
+            left = [wide[pl.ds(e * COLS + j + i, 32, stride=48), :] for i in range(2)]
+            at = (e, slice(None), pl.ds(j * LANES, 2 * LANES))
+            right = [r[at] for r in (own, ahead, opposite, back)]
             total += lax.dot_general(
-                jnp.concatenate(left, axis=1),
-                right,
+                jnp.concatenate(left, axis=1).astype(jnp.bfloat16),
+                jnp.concatenate(right, axis=0),
                 (((1,), (1,)), ((), ())),
                 preferred_element_type=jnp.float32,
             )
-    total = total * (6144 ** (-0.5))
-    for e in range(2):
-        own = total[:, e * 64 : (e + 1) * 64]
-        for x in range(4):
-            for z0 in range(2):
-                row = (x * 2 + z0) * 16 + e * 8
-                out[e, pl.ds(x * 16 + z0, 8, stride=2), :] = own[row : row + 8]
+        totals.append(total)
+    for k in range(4):
+        x = lax.rem(me + 4 - k * step, 4)
+        for t in range(2):
+            pair = [w[t * 16 : (t + 1) * 16, k * 64 : (k + 1) * 64] for w in totals]
+            out[x * 2 + t] = jnp.concatenate(pair, axis=1)
+
+
+def end_kernel(parts, out):
+    scale = 6144 ** (-0.5)
+    for x in range(4):
+        total = (parts[2 * x] + parts[2 * x + 1]) * scale
+        for e in range(2):
+            out[e, x * 16 : (x + 1) * 16, :] = total[:, e * 64 : (e + 1) * 64]
 
 
 def call(kernel, out_shape, in_specs, scratch=(), out_specs=None):
@@ -151,6 +161,13 @@
     )
 
 
+def shift(array, by):
+    pairs = [
+        (x * 2 + t, (x + (by if t == 0 else -by)) % 4 * 2 + t) for x in range(4) for t in range(2)
+    ]
+    return lax.ppermute(array, ("x", "tensor"), pairs)
+
+
 def swap(array, axes):
     return lax.all_to_all(array, axes, 0, 0, tiled=True)
 
@@ -160,7 +177,6 @@
     shape = jax.ShapeDtypeStruct
     mine = grad_hidden[0, 0]
     other = lax.ppermute(mine, "tensor", [(0, 1), (1, 0)])
-    far_inputs = lax.ppermute(next_rows[0], "tensor", [(0, 1), (1, 0)])
     held, hidden, inside = call(
         stage_kernel,
         [
@@ -187,25 +203,30 @@
         out_specs=HBM,
     )(hidden, other, inside, held)
     parts = swap(parts, NEAR)
+    parts, inputs = lax.optimization_barrier((parts, next_rows[0]))
+    ahead, back = shift(inputs, 1), shift(inputs, -1)
+    opposite = shift(ahead, 1)
     parts = call(
         near_sum_kernel,
         shape((16, 48, LANES), bf16),
-        [VMEM, HBM],
+        [VMEM],
         [pltpu.VMEM((COLS * 32, LANES), f32)],
-    )(parts, far_inputs)
+    )(parts)
     parts = swap(parts, FAR)
     state = [a.reshape(2, 48, LANES) for a in (master, moment1, moment2)]
     *new, send = call(
-        step_kernel, [shape((2, 48, LANES), f32)] * 3 + [shape((8, 96, LANES), bf16)], [VMEM] * 4
+        step_kernel,
+        [shape((2, 48, LANES), f32)] * 3 + [pltpu.HBM((32, 48, LANES), bf16)],
+        [VMEM] * 4,
+        [pltpu.VMEM((32, 48, LANES), bf16), pltpu.SemaphoreType.DMA((2,))],
+        out_specs=[VMEM] * 3 + [HBM],
     )(parts, *state)
-    got = swap(send, ("h", "z1"))
-    got = call(
-        turn_kernel, shape((8, 48, 16, LANES), bf16), [VMEM], [pltpu.VMEM((8 * 96, LANES), f32)]
-    )(got)
-    got = swap(got, NEAR)
-    gates = call(gate_kernel, shape((2, 64, 64), f32), [VMEM] * 3)(
-        got, next_rows[0], far_inputs
-    )
+    got = swap(send, ("tensor", "h", "z1", "z0"))
+    gates = call(
+        gate_kernel, shape((8, 16, LANES), f32), [VMEM] * 5, [pltpu.VMEM((32 * 48, LANES), f32)]
+    )(got, inputs, ahead, opposite, back)
+    gates = swap(gates, ("x", "tensor"))
+    gates = call(end_kernel, shape((2, 64, 64), f32), [VMEM])(gates)
     return (*[a.reshape(2, 1, 1, 6144) for a in new], gates[None])
 
 

time: 108 us -> 105 us (0.972)
  blocking collectives: 70.1 us -> 38.1 us
  starting transfers between devices: 10.4 us -> 28.6 us
  waiting for transfers between devices: 19.7 us -> 28.1 us
  Pallas kernels: 6.57 us -> 8.34 us
    all_to_all x3 -> x2, blocking collectives: 70.1 us -> 38.1 us  [swap(): return lax.all_to_all(array, axes, 0, 0, tiled=True)]
    all_to_all x1 -> x2, starting transfers between devices: 6.25 us -> 17.8 us  [swap(): return lax.all_to_all(array, axes, 0, 0, tiled=True)]
    all_to_all x1 -> x2, waiting for transfers between devices: 17.7 us -> 28.1 us  [swap(): return lax.all_to_all(array, axes, 0, 0, tiled=True)]
    ppermute x1 -> x3, starting transfers between devices: 2.26 us -> 8.96 us  [shift(): return lax.ppermute(array, ('x', 'tensor'), pairs)]
    ppermute x1 -> x3, waiting for transfers between devices: 2.05 us -> 0.04 us  [shift(): return lax.ppermute(array, ('x', 'tensor'), pairs)]
    pallas_call x4, Pallas kernels: 2.66 us -> 4.41 us  [the longest x1 1.46 us: per_device(): call(step_kernel, [shape((2, 48, LANES), f32)] * 3 + [pltpu.HBM((32, 48,...]
  transfers between devices with their start and end apart: 3 -> 6, of which waited for: 2 -> 2; matrix products, arithmetic and copies ran while one was open for 0% -> 0% of each run, Pallas kernels for 2% -> 4%
where the time goes in v3:
time: 105 us; the launch traced here: 104 us
  blocking collectives  38.1 us (36%)
  starting transfers between devices  28.6 us (27%)
  waiting for transfers between devices  28.1 us (27%)
  Pallas kernels  8.34 us (8%)
    all_to_all x2, blocking collectives, swap(): return lax.all_to_all(array, axes, 0, 0, tiled=True)  38.1 us
    all_to_all x2, waiting for transfers between devices, swap(): return lax.all_to_all(array, axes, 0, 0, tiled=True)  28.1 us
    all_to_all x2, starting transfers between devices, swap(): return lax.all_to_all(array, axes, 0, 0, tiled=True)  17.8 us
    ppermute x3, starting transfers between devices, shift(): return lax.ppermute(array, ('x', 'tensor'), pairs)  8.96 us
  transfers between devices with their start and end apart: 6, of which 2 were waited for; matrix products, arithmetic and copies ran while one was open for 0% of the time, Pallas kernels for 4%

profile of v3, /device:TPU:8, one launch (start us, length us, event | category | flops | bytes accessed | tf_op | source)
XLA Modules:
  0.0 104.1 jit_solution(4903308103791698866)
XLA Ops:
  0.6 1.9 %collective-permute-start = (bf16[64,512]{1,0:T(8,128)(2,1)}, bf16[64,512]{1,0:T(8,128)(2,1)S(1)}, u32[]{:S(2)}, u32[]{:S(2)}) collective-permute-start(bf16[64,512]{1,0:T(8,128)(2,1)} %bitcast.17), channel_id=1, source_target_pairs={{0,1},{1,0},{2,3},{3,2},{4,5},{5,4},{6,7},{7,6},{8,9},{9,8},{10,11... | collective-permute-start | bytes 196616 | tf_op jit(solution)/shard_map/ppermute | solution.py:179
  2.6 2.0 %shard_map.111 = (bf16[512,3072]{1,0:T(8,128)(2,1)S(1)}, bf16[64,512]{1,0:T(8,128)(2,1)S(1)}, bf16[256,512]{1,0:T(8,128)(2,1)S(1)}) custom-call(s32[1,2]{1,0:T(1,128)} %starts.1, s32[1,2]{1,0:T(1,128)} %sizes.1, bf16[64,512]{1,0:T(8,128)(2,1)} %bitcast.18, bf16[512,3072]{1,0:T(8,128)(2,1)} %bitcast.16), custom_call_target="tpu_custom_call" | custom-call | tf_op jit(solution)/shard_map/pallas_call | solution.py:180
  4.5 0.0 collective-permute-done.other
  4.5 0.0 copy-start
  4.6 2.0 %shard_map.112 = bf16[8,24,32,128]{3,2,1,0:T(8,128)(2,1)} custom-call(bf16[64,512]{1,0:T(8,128)(2,1)S(1)} %get-tuple-element.13.mine, bf16[64,512]{1,0:T(8,128)(2,1)S(1)} %collective-permute-done.other, bf16[256,512]{1,0:T(8,128)(2,1)S(1)} %get-tuple-element.14.inside, bf16[512,3072]{1,0:T(8,128)(2,1)S(1)} %get-tuple-element.15.rows), custom_call_target="tpu_custom_call" | custom-call | tf_op jit(solution)/shard_map/pallas_call | solution.py:195
  6.5 0.0 copy-start.1
  6.5 0.0 copy-start.2
  6.6 0.0 copy-start.3
  6.6 28.2 %all_to_all.20.parts = bf16[8,24,32,128]{3,2,1,0:T(8,128)(2,1)S(1)} all-to-all(bf16[8,24,32,128]{3,2,1,0:T(8,128)(2,1)} %shard_map.112), channel_id=1, replica_groups=mesh['x'=4,'h'=2,'z1'=4,'z0'=2,'expert'=4,'tensor'=2] {'x','z0'}, dimensions={0} | all-to-all | bytes 3145728 | tf_op jit(solution)/shard_map/all_to_all | solution.py:172
  34.8 2.1 %collective-permute-start.1 = (bf16[2,64,3072]{2,1,0:T(8,128)(2,1)S(1)}, bf16[2,64,3072]{2,1,0:T(8,128)(2,1)S(1)}, u32[]{:S(2)}, u32[]{:S(2)}) collective-permute-start(bf16[2,64,3072]{2,1,0:T(8,128)(2,1)S(1)} %bitcast.10), channel_id=1, source_target_pairs={{0,128},{1,385},{128,256},{129,1},{256,384},{257,129},{384,0},{385... | collective-permute-start | bytes 2359304 | tf_op jit(solution)/shard_map/ppermute | solution.py:168
  36.9 1.1 %shard_map.113 = bf16[16,48,128]{2,1,0:T(8,128)(2,1)} custom-call(bf16[8,24,32,128]{3,2,1,0:T(8,128)(2,1)S(1)} %all_to_all.20.parts), custom_call_target="tpu_custom_call" | custom-call | tf_op jit(solution)/shard_map/pallas_call | solution.py:209
  38.0 13.9 %all-to-all-start.1 = ((bf16[16,48,128]{2,1,0:T(8,128)(2,1)}), bf16[16,48,128]{2,1,0:T(8,128)(2,1)S(1)}, u32[]{:S(2)}, u32[]{:S(2)}) async-start(bf16[16,48,128]{2,1,0:T(8,128)(2,1)} %shard_map.113), calls=%async_computation.1 | async-start | bytes 393216 | tf_op jit(solution)/shard_map/all_to_all | solution.py:172
  51.9 4.9 %collective-permute-start.3 = (bf16[2,64,3072]{2,1,0:T(8,128)(2,1)S(1)}, bf16[2,64,3072]{2,1,0:T(8,128)(2,1)S(1)}, u32[]{:S(2)}, u32[]{:S(2)}) collective-permute-start(bf16[2,64,3072]{2,1,0:T(8,128)(2,1)S(1)} %bitcast.11), channel_id=1, source_target_pairs={{0,384},{1,129},{128,0},{129,257},{256,128},{257,385},{384,256},{3... | collective-permute-start | bytes 2359304 | tf_op jit(solution)/shard_map/ppermute | solution.py:168
  56.8 0.0 collective-permute-done.1.ahead
  56.8 1.9 %collective-permute-start.2 = (bf16[2,64,3072]{2,1,0:T(8,128)(2,1)S(1)}, bf16[2,64,3072]{2,1,0:T(8,128)(2,1)S(1)}, u32[]{:S(2)}, u32[]{:S(2)}) collective-permute-start(bf16[2,64,3072]{2,1,0:T(8,128)(2,1)S(1)} %collective-permute-done.1.ahead), channel_id=1, source_target_pairs={{0,128},{1,385},{128,256},{129,1},{256,384},{257,129},{384,0},{385... | collective-permute-start | bytes 2359304 | tf_op jit(solution)/shard_map/ppermute | solution.py:168
  58.8 9.1 %all-to-all-done.1.parts = bf16[16,48,128]{2,1,0:T(8,128)(2,1)S(1)} async-done(((bf16[16,48,128]{2,1,0:T(8,128)(2,1)}), bf16[16,48,128]{2,1,0:T(8,128)(2,1)S(1)}, u32[]{:S(2)}, u32[]{:S(2)}) %all-to-all-start.1) | async-done | bytes 196640 | tf_op jit(solution)/shard_map/all_to_all | solution.py:172
  67.9 1.5 %shard_map.114 = (f32[2,48,128]{2,1,0:T(8,128)}, f32[2,48,128]{2,1,0:T(8,128)}, f32[2,48,128]{2,1,0:T(8,128)}, bf16[32,48,128]{2,1,0:T(8,128)(2,1)}) custom-call(bf16[16,48,128]{2,1,0:T(8,128)(2,1)S(1)} %all-to-all-done.1.parts, f32[2,48,128]{2,1,0:T(8,128)S(1)} %bitcast.13, f32[2,48,128]{2,1,0:T(8,128)S(1)} %bitcast.14, f32[2,48,128]{2,1,0:T(8,128)S(1)} %bitcast.15), custom_call_target="tpu_custom_call" | custom-call | tf_op jit(solution)/shard_map/pallas_call | solution.py:217
  69.4 3.9 %all-to-all-start.2 = ((bf16[32,48,128]{2,1,0:T(8,128)(2,1)}), bf16[32,48,128]{2,1,0:T(8,128)(2,1)S(1)}, u32[]{:S(2)}, u32[]{:S(2)}) async-start(bf16[32,48,128]{2,1,0:T(8,128)(2,1)} %get-tuple-element.20), calls=%async_computation.2 | async-start | bytes 786432 | tf_op jit(solution)/shard_map/all_to_all | solution.py:172
  73.3 0.0 collective-permute-done.3.back
  73.3 18.9 %all-to-all-done.2.got = bf16[32,48,128]{2,1,0:T(8,128)(2,1)S(1)} async-done(((bf16[32,48,128]{2,1,0:T(8,128)(2,1)}), bf16[32,48,128]{2,1,0:T(8,128)(2,1)S(1)}, u32[]{:S(2)}, u32[]{:S(2)}) %all-to-all-start.2) | async-done | bytes 393248 | tf_op jit(solution)/shard_map/all_to_all | solution.py:172
  92.3 0.0 collective-permute-done.2.opposite
  92.3 1.2 %shard_map.115 = f32[8,16,128]{2,1,0:T(8,128)S(1)} custom-call(bf16[32,48,128]{2,1,0:T(8,128)(2,1)S(1)} %all-to-all-done.2.got, bf16[2,64,3072]{2,1,0:T(8,128)(2,1)S(1)} %bitcast.12, bf16[2,64,3072]{2,1,0:T(8,128)(2,1)S(1)} %collective-permute-done.1.ahead, bf16[2,64,3072]{2,1,0:T(8,128)(2,1)S(1)} %collective-permute-done.2.opposite, ...), custom_call_target="tpu_custom_call" | custom-call | tf_op jit(solution)/shard_map/pallas_call | solution.py:225
  93.4 9.9 %all_to_all.21.parts = f32[8,16,128]{2,1,0:T(8,128)S(1)} all-to-all(f32[8,16,128]{2,1,0:T(8,128)S(1)} %shard_map.115), channel_id=1, replica_groups=mesh['x'=4,'h'=2,'z1'=4,'z0'=2,'expert'=4,'tensor'=2] {'x','tensor'}, dimensions={0} | all-to-all | bytes 131072 | tf_op jit(solution)/shard_map/all_to_all | solution.py:172
  103.3 0.7 shard_map.116
  (4 shorter events, 0.0 us)
Async XLA Ops:
  0.6 3.9 %collective-permute-start = (bf16[64,512]{1,0:T(8,128)(2,1)}, bf16[64,512]{1,0:T(8,128)(2,1)S(1)}, u32[]{:S(2)}, u32[]{:S(2)}) collective-permute-start(bf16[64,512]{1,0:T(8,128)(2,1)} %bitcast.17), channel_id=1, source_target_pairs={{0,1},{1,0},{2,3},{3,2},{4,5},{5,4},{6,7},{7,6},{8,9},{9,8},{10,11... | collective-permute-start | bytes 196616 | tf_op jit(solution)/shard_map/ppermute | solution.py:179
  4.5 30.3 %copy-start = (bf16[1,2,64,3072]{3,2,1,0:T(8,128)(2,1)S(1)}, bf16[1,2,64,3072]{3,2,1,0:T(8,128)(2,1)}, u32[]{:S(2)}) copy-start(bf16[1,2,64,3072]{3,2,1,0:T(8,128)(2,1)} %param.15) | copy-start | bytes 2359300
  6.5 61.4 %copy-start.1 = (f32[2,1,1,6144]{3,2,1,0:T(1,128)S(1)}, f32[2,1,1,6144]{3,2,1,0:T(1,128)}, u32[]{:S(2)}) copy-start(f32[2,1,1,6144]{3,2,1,0:T(1,128)} %param.12) | copy-start | bytes 147460
  6.5 61.4 %copy-start.2 = (f32[2,1,1,6144]{3,2,1,0:T(1,128)S(1)}, f32[2,1,1,6144]{3,2,1,0:T(1,128)}, u32[]{:S(2)}) copy-start(f32[2,1,1,6144]{3,2,1,0:T(1,128)} %param.13) | copy-start | bytes 147460
  6.6 61.3 %copy-start.3 = (f32[2,1,1,6144]{3,2,1,0:T(1,128)S(1)}, f32[2,1,1,6144]{3,2,1,0:T(1,128)}, u32[]{:S(2)}) copy-start(f32[2,1,1,6144]{3,2,1,0:T(1,128)} %param.14) | copy-start | bytes 147460
  34.8 22.0 %collective-permute-start.1 = (bf16[2,64,3072]{2,1,0:T(8,128)(2,1)S(1)}, bf16[2,64,3072]{2,1,0:T(8,128)(2,1)S(1)}, u32[]{:S(2)}, u32[]{:S(2)}) collective-permute-start(bf16[2,64,3072]{2,1,0:T(8,128)(2,1)S(1)} %bitcast.10), channel_id=1, source_target_pairs={{0,128},{1,385},{128,256},{129,1},{256,384},{257,129},{384,0},{385... | collective-permute-start | bytes 2359304 | tf_op jit(solution)/shard_map/ppermute | solution.py:168
  38.0 29.9 %all-to-all-start.1 = ((bf16[16,48,128]{2,1,0:T(8,128)(2,1)}), bf16[16,48,128]{2,1,0:T(8,128)(2,1)S(1)}, u32[]{:S(2)}, u32[]{:S(2)}) async-start(bf16[16,48,128]{2,1,0:T(8,128)(2,1)} %shard_map.113), calls=%async_computation.1 | async-start | bytes 393216 | tf_op jit(solution)/shard_map/all_to_all | solution.py:172
  51.9 21.4 %collective-permute-start.3 = (bf16[2,64,3072]{2,1,0:T(8,128)(2,1)S(1)}, bf16[2,64,3072]{2,1,0:T(8,128)(2,1)S(1)}, u32[]{:S(2)}, u32[]{:S(2)}) collective-permute-start(bf16[2,64,3072]{2,1,0:T(8,128)(2,1)S(1)} %bitcast.11), channel_id=1, source_target_pairs={{0,384},{1,129},{128,0},{129,257},{256,128},{257,385},{384,256},{3... | collective-permute-start | bytes 2359304 | tf_op jit(solution)/shard_map/ppermute | solution.py:168
  56.8 35.4 %collective-permute-start.2 = (bf16[2,64,3072]{2,1,0:T(8,128)(2,1)S(1)}, bf16[2,64,3072]{2,1,0:T(8,128)(2,1)S(1)}, u32[]{:S(2)}, u32[]{:S(2)}) collective-permute-start(bf16[2,64,3072]{2,1,0:T(8,128)(2,1)S(1)} %collective-permute-done.1.ahead), channel_id=1, source_target_pairs={{0,128},{1,385},{128,256},{129,1},{256,384},{257,129},{384,0},{385... | collective-permute-start | bytes 2359304 | tf_op jit(solution)/shard_map/ppermute | solution.py:168
  69.4 22.9 %all-to-all-start.2 = ((bf16[32,48,128]{2,1,0:T(8,128)(2,1)}), bf16[32,48,128]{2,1,0:T(8,128)(2,1)S(1)}, u32[]{:S(2)}, u32[]{:S(2)}) async-start(bf16[32,48,128]{2,1,0:T(8,128)(2,1)} %get-tuple-element.20), calls=%async_computation.2 | async-start | bytes 786432 | tf_op jit(solution)/shard_map/all_to_all | solution.py:172

commit v4 on v3

--- a/solution.py
+++ b/solution.py
@@ -22,6 +22,8 @@
 BLOCK = 512
 PIECES = 3072 // BLOCK
 GROUP = BLOCK // LANES
+LATE = 3_000_000_000
+LATER = 3_000_000_000
 
 VMEM = pl.BlockSpec(memory_space=pltpu.VMEM)
 HBM = pl.BlockSpec(memory_space=pltpu.HBM)
@@ -59,11 +61,7 @@
         copy.wait()
 
 
-def grad_kernel(mine, other, inside, rows, out, ready, sems):
-    stores = [
-        pltpu.make_async_copy(ready.at[k], out.at[:, pl.ds(k * GROUP, GROUP)], sems.at[k])
-        for k in range(PIECES)
-    ]
+def grad_kernel(mine, other, inside, rows, out):
     me = lax.axis_index("tensor")
     i = lax.broadcasted_iota(jnp.int32, (256, 64), 0)
     c = lax.broadcasted_iota(jnp.int32, (256, 64), 1)
@@ -78,18 +76,24 @@
             masked, rows[:, k * BLOCK : (k + 1) * BLOCK], preferred_element_type=jnp.float32
         ).astype(jnp.bfloat16)
         for j in range(GROUP):
-            ready[k, :, j] = piece[:, j * LANES : (j + 1) * LANES].reshape(8, 32, LANES)
-        stores[k].start()
-    for copy in stores:
-        copy.wait()
-
-
-def near_sum_kernel(parts, out, total):
+            block = piece[:, j * LANES : (j + 1) * LANES]
+            out[:, k * GROUP + j] = block.reshape(8, 32, LANES)
+
+
+def near_sum_kernel(parts, out, total, ready, sems):
+    copies = [
+        pltpu.make_async_copy(ready.at[pl.ds(k * 4, 4)], out.at[pl.ds(k * 4, 4)], sems.at[k])
+        for k in range(4)
+    ]
     for j in range(COLS):
         total[j * 32 : (j + 1) * 32] = jnp.sum(parts[:, j].astype(jnp.float32), axis=0)
-    for d in range(16):
-        pair = [total[pl.ds(2 * d + e, COLS, stride=32), :] for e in range(2)]
-        out[d] = jnp.concatenate(pair, axis=0).astype(jnp.bfloat16)
+    for k in range(4):
+        for d in range(4 * k, 4 * k + 4):
+            pair = [total[pl.ds(2 * d + e, COLS, stride=32), :] for e in range(2)]
+            ready[d] = jnp.concatenate(pair, axis=0).astype(jnp.bfloat16)
+        copies[k].start()
+    for copy in copies:
+        copy.wait()
 
 
 def step_kernel(parts, master, first, second, new_master, new_first, new_second, send, block, sems):
@@ -115,20 +119,27 @@
         copy.wait()
 
 
-def gate_kernel(got, own, ahead, opposite, back, out, wide):
+def turn_kernel(got, unused, out, wide):
+    del unused
+    for r in range(32):
+        wide[r * 48 : (r + 1) * 48] = got[r].astype(jnp.float32)
+    for k in range(48):
+        out[k] = wide[pl.ds(k, 32, stride=48), :].astype(jnp.bfloat16)
+
+
+def gate_kernel(weights, own, ahead, opposite, back, out):
     me = lax.axis_index("x")
     step = 1 - 2 * lax.axis_index("tensor")
-    for r in range(32):
-        wide[r * 48 : (r + 1) * 48] = got[r].astype(jnp.float32)
+    inputs = (own, ahead, opposite, back)
     totals = []
     for e in range(2):
         total = jnp.zeros((32, 256), jnp.float32)
         for j in range(0, COLS, 2):
-            left = [wide[pl.ds(e * COLS + j + i, 32, stride=48), :] for i in range(2)]
+            left = [weights[e * COLS + j + i] for i in range(2)]
             at = (e, slice(None), pl.ds(j * LANES, 2 * LANES))
-            right = [r[at] for r in (own, ahead, opposite, back)]
+            right = [r[at] for r in inputs]
             total += lax.dot_general(
-                jnp.concatenate(left, axis=1).astype(jnp.bfloat16),
+                jnp.concatenate(left, axis=1),
                 jnp.concatenate(right, axis=0),
                 (((1,), (1,)), ((), ())),
                 preferred_element_type=jnp.float32,
@@ -149,7 +160,7 @@
             out[e, x * 16 : (x + 1) * 16, :] = total[:, e * 64 : (e + 1) * 64]
 
 
-def call(kernel, out_shape, in_specs, scratch=(), out_specs=None):
+def call(kernel, out_shape, in_specs, scratch=(), out_specs=None, flops=None):
     many = isinstance(out_shape, (list, tuple))
     return pl.pallas_call(
         kernel,
@@ -157,6 +168,8 @@
         in_specs=in_specs,
         out_specs=out_specs or ([VMEM] * len(out_shape) if many else VMEM),
         scratch_shapes=list(scratch),
+        cost_estimate=flops
+        and pl.CostEstimate(flops=flops, bytes_accessed=0, transcendentals=0),
         compiler_params=pltpu.CompilerParams(vmem_limit_bytes=16 << 20),
     )
 
@@ -194,23 +207,22 @@
     )
     parts = call(
         grad_kernel,
-        pltpu.HBM((8, COLS, 32, LANES), bf16),
+        pltpu.VMEM((8, COLS, 32, LANES), bf16),
         [VMEM] * 4,
-        [
-            pltpu.VMEM((PIECES, 8, GROUP, 32, LANES), bf16),
-            pltpu.SemaphoreType.DMA((PIECES,)),
-        ],
-        out_specs=HBM,
     )(hidden, other, inside, held)
     parts = swap(parts, NEAR)
     parts, inputs = lax.optimization_barrier((parts, next_rows[0]))
     ahead, back = shift(inputs, 1), shift(inputs, -1)
-    opposite = shift(ahead, 1)
     parts = call(
         near_sum_kernel,
-        shape((16, 48, LANES), bf16),
+        pltpu.HBM((16, 48, LANES), bf16),
         [VMEM],
-        [pltpu.VMEM((COLS * 32, LANES), f32)],
+        [
+            pltpu.VMEM((COLS * 32, LANES), f32),
+            pltpu.VMEM((16, 48, LANES), bf16),
+            pltpu.SemaphoreType.DMA((4,)),
+        ],
+        out_specs=HBM,
     )(parts)
     parts = swap(parts, FAR)
     state = [a.reshape(2, 48, LANES) for a in (master, moment1, moment2)]
@@ -220,11 +232,21 @@
         [VMEM] * 4,
         [pltpu.VMEM((32, 48, LANES), bf16), pltpu.SemaphoreType.DMA((2,))],
         out_specs=[VMEM] * 3 + [HBM],
+        flops=LATE,
     )(parts, *state)
     got = swap(send, ("tensor", "h", "z1", "z0"))
-    gates = call(
-        gate_kernel, shape((8, 16, LANES), f32), [VMEM] * 5, [pltpu.VMEM((32 * 48, LANES), f32)]
-    )(got, inputs, ahead, opposite, back)
+    relayed, new[0] = lax.optimization_barrier((ahead, new[0]))
+    opposite = shift(relayed, 1)
+    weights = call(
+        turn_kernel,
+        shape((48, 32, LANES), bf16),
+        [VMEM, HBM],
+        [pltpu.VMEM((32 * 48, LANES), f32)],
+        flops=LATER,
+    )(got, back)
+    gates = call(gate_kernel, shape((8, 16, LANES), f32), [VMEM] * 5)(
+        weights, inputs, ahead, opposite, back
+    )
     gates = swap(gates, ("x", "tensor"))
     gates = call(end_kernel, shape((2, 64, 64), f32), [VMEM])(gates)
     return (*[a.reshape(2, 1, 1, 6144) for a in new], gates[None])

time: 105 us -> 99.9 us (0.951)
  blocking collectives: 38.1 us -> 36 us
  waiting for transfers between devices: 28.1 us -> 26.1 us
    all_to_all x2, blocking collectives: 38.1 us -> 36 us  [swap(): return lax.all_to_all(array, axes, 0, 0, tiled=True)]
    all_to_all x2, waiting for transfers between devices: 28.1 us -> 26 us  [swap(): return lax.all_to_all(array, axes, 0, 0, tiled=True)]
    pallas_call x3 -> x4, Pallas kernels: 4.21 us -> 3.6 us  [the longest x1 1.19 us: per_device(): call(grad_kernel, pltpu.VMEM((8, COLS, 32, LANES), bf16), [VMEM] * 4)]
  transfers between devices with their start and end apart: 6 -> 6, of which waited for: 2 -> 3; matrix products, arithmetic and copies ran while one was open for 0% -> 0% of each run, Pallas kernels for 4% -> 4%
where the time goes in v4:
time: 99.9 us; the launch traced here: 99.4 us
  blocking collectives  36 us (36%)
  starting transfers between devices  28.7 us (29%)
  waiting for transfers between devices  26.1 us (26%)
  Pallas kernels  7.74 us (8%)
    all_to_all x2, blocking collectives, swap(): return lax.all_to_all(array, axes, 0, 0, tiled=True)  36 us
    all_to_all x2, waiting for transfers between devices, swap(): return lax.all_to_all(array, axes, 0, 0, tiled=True)  26 us
    all_to_all x2, starting transfers between devices, swap(): return lax.all_to_all(array, axes, 0, 0, tiled=True)  17.8 us
    ppermute x3, starting transfers between devices, shift(): return lax.ppermute(array, ('x', 'tensor'), pairs)  9.05 us
  transfers between devices with their start and end apart: 6, of which 3 were waited for; matrix products, arithmetic and copies ran while one was open for 0% of the time, Pallas kernels for 4%

profile of v4, /device:TPU:8, one launch (start us, length us, event | category | flops | bytes accessed | tf_op | source)
XLA Modules:
  0.0 99.4 jit_solution(16375682154753796617)
XLA Ops:
  0.6 1.9 %collective-permute-start = (bf16[64,512]{1,0:T(8,128)(2,1)}, bf16[64,512]{1,0:T(8,128)(2,1)S(1)}, u32[]{:S(2)}, u32[]{:S(2)}) collective-permute-start(bf16[64,512]{1,0:T(8,128)(2,1)} %bitcast.17), channel_id=1, source_target_pairs={{0,1},{1,0},{2,3},{3,2},{4,5},{5,4},{6,7},{7,6},{8,9},{9,8},{10,11... | collective-permute-start | bytes 196616 | tf_op jit(solution)/shard_map/ppermute | solution.py:192
  2.6 2.0 %shard_map.111 = (bf16[512,3072]{1,0:T(8,128)(2,1)S(1)}, bf16[64,512]{1,0:T(8,128)(2,1)S(1)}, bf16[256,512]{1,0:T(8,128)(2,1)S(1)}) custom-call(s32[1,2]{1,0:T(1,128)} %starts.1, s32[1,2]{1,0:T(1,128)} %sizes.1, bf16[64,512]{1,0:T(8,128)(2,1)} %bitcast.18, bf16[512,3072]{1,0:T(8,128)(2,1)} %bitcast.16), custom_call_target="tpu_custom_call" | custom-call | tf_op jit(solution)/shard_map/pallas_call | solution.py:193
  4.5 0.0 collective-permute-done.other
  4.5 1.2 %shard_map.112 = bf16[8,24,32,128]{3,2,1,0:T(8,128)(2,1)S(1)} custom-call(bf16[64,512]{1,0:T(8,128)(2,1)S(1)} %get-tuple-element.15.mine, bf16[64,512]{1,0:T(8,128)(2,1)S(1)} %collective-permute-done.other, bf16[256,512]{1,0:T(8,128)(2,1)S(1)} %get-tuple-element.16.inside, bf16[512,3072]{1,0:T(8,128)(2,1)S(1)} %get-tuple-element.17.rows), custom_call_target="tpu_custom_call" | custom-call | tf_op jit(solution)/shard_map/pallas_call | solution.py:208
  5.7 0.0 copy-start
  5.8 0.0 copy-start.1
  5.8 0.0 copy-start.2
  5.8 0.0 copy-start.3
  5.8 28.0 %all_to_all.20.parts = bf16[8,24,32,128]{3,2,1,0:T(8,128)(2,1)S(1)} all-to-all(bf16[8,24,32,128]{3,2,1,0:T(8,128)(2,1)S(1)} %shard_map.112), channel_id=1, replica_groups=mesh['x'=4,'h'=2,'z1'=4,'z0'=2,'expert'=4,'tensor'=2] {'x','z0'}, dimensions={0} | all-to-all | bytes 3145728 | tf_op jit(solution)/shard_map/all_to_all | solution.py:185
  33.8 1.0 %shard_map.113 = bf16[16,48,128]{2,1,0:T(8,128)(2,1)} custom-call(bf16[8,24,32,128]{3,2,1,0:T(8,128)(2,1)S(1)} %all_to_all.20.parts), custom_call_target="tpu_custom_call" | custom-call | tf_op jit(solution)/shard_map/pallas_call | solution.py:216
  34.9 13.9 %all-to-all-start.1 = ((bf16[16,48,128]{2,1,0:T(8,128)(2,1)}), bf16[16,48,128]{2,1,0:T(8,128)(2,1)S(1)}, u32[]{:S(2)}, u32[]{:S(2)}) async-start(bf16[16,48,128]{2,1,0:T(8,128)(2,1)} %shard_map.113), calls=%async_computation.1 | async-start | bytes 393216 | tf_op jit(solution)/shard_map/all_to_all | solution.py:185
  48.8 2.1 %collective-permute-start.1 = (bf16[2,64,3072]{2,1,0:T(8,128)(2,1)S(1)}, bf16[2,64,3072]{2,1,0:T(8,128)(2,1)S(1)}, u32[]{:S(2)}, u32[]{:S(2)}) collective-permute-start(bf16[2,64,3072]{2,1,0:T(8,128)(2,1)S(1)} %bitcast.10), channel_id=1, source_target_pairs={{0,128},{1,385},{128,256},{129,1},{256,384},{257,129},{384,0},{385... | collective-permute-start | bytes 2359304 | tf_op jit(solution)/shard_map/ppermute | solution.py:181
  50.9 4.9 %collective-permute-start.2 = (bf16[2,64,3072]{2,1,0:T(8,128)(2,1)S(1)}, bf16[2,64,3072]{2,1,0:T(8,128)(2,1)S(1)}, u32[]{:S(2)}, u32[]{:S(2)}) collective-permute-start(bf16[2,64,3072]{2,1,0:T(8,128)(2,1)S(1)} %bitcast.11), channel_id=1, source_target_pairs={{0,384},{1,129},{128,0},{129,257},{256,128},{257,385},{384,256},{3... | collective-permute-start | bytes 2359304 | tf_op jit(solution)/shard_map/ppermute | solution.py:181
  55.8 8.9 %all-to-all-done.1.parts = bf16[16,48,128]{2,1,0:T(8,128)(2,1)S(1)} async-done(((bf16[16,48,128]{2,1,0:T(8,128)(2,1)}), bf16[16,48,128]{2,1,0:T(8,128)(2,1)S(1)}, u32[]{:S(2)}, u32[]{:S(2)}) %all-to-all-start.1) | async-done | bytes 196640 | tf_op jit(solution)/shard_map/all_to_all | solution.py:185
  64.8 1.5 %shard_map.114 = (f32[2,48,128]{2,1,0:T(8,128)}, f32[2,48,128]{2,1,0:T(8,128)}, f32[2,48,128]{2,1,0:T(8,128)}, bf16[32,48,128]{2,1,0:T(8,128)(2,1)}) custom-call(bf16[16,48,128]{2,1,0:T(8,128)(2,1)S(1)} %all-to-all-done.1.parts, f32[2,48,128]{2,1,0:T(8,128)S(1)} %bitcast.13, f32[2,48,128]{2,1,0:T(8,128)S(1)} %bitcast.14, f32[2,48,128]{2,1,0:T(8,128)S(1)} %bitcast.15), custom_call_target="tpu_custom_call" | custom-call | flops 3000000000 | tf_op jit(solution)/shard_map/pallas_call | solution.py:229
  66.2 3.9 %all-to-all-start.2 = ((bf16[32,48,128]{2,1,0:T(8,128)(2,1)}), bf16[32,48,128]{2,1,0:T(8,128)(2,1)S(1)}, u32[]{:S(2)}, u32[]{:S(2)}) async-start(bf16[32,48,128]{2,1,0:T(8,128)(2,1)} %get-tuple-element.24), calls=%async_computation.2 | async-start | bytes 786432 | tf_op jit(solution)/shard_map/all_to_all | solution.py:185
  70.1 0.1 collective-permute-done.1.ahead
  70.3 2.0 %collective-permute-start.3 = (bf16[2,64,3072]{2,1,0:T(8,128)(2,1)S(1)}, bf16[2,64,3072]{2,1,0:T(8,128)(2,1)S(1)}, u32[]{:S(2)}, u32[]{:S(2)}) collective-permute-start(bf16[2,64,3072]{2,1,0:T(8,128)(2,1)S(1)} %collective-permute-done.1.ahead), channel_id=1, source_target_pairs={{0,128},{1,385},{128,256},{129,1},{256,384},{257,129},{384,0},{385... | collective-permute-start | bytes 2359304 | tf_op jit(solution)/shard_map/ppermute | solution.py:181
  72.3 0.0 collective-permute-done.2.unused.back
  72.3 17.0 %all-to-all-done.2.got = bf16[32,48,128]{2,1,0:T(8,128)(2,1)S(1)} async-done(((bf16[32,48,128]{2,1,0:T(8,128)(2,1)}), bf16[32,48,128]{2,1,0:T(8,128)(2,1)S(1)}, u32[]{:S(2)}, u32[]{:S(2)}) %all-to-all-start.2) | async-done | bytes 393248 | tf_op jit(solution)/shard_map/all_to_all | solution.py:185
  89.3 0.3 shard_map.115.weights
  89.6 1.1 %shard_map.116 = f32[8,16,128]{2,1,0:T(8,128)S(1)} custom-call(bf16[48,32,128]{2,1,0:T(8,128)(2,1)S(1)} %shard_map.115.weights, bf16[2,64,3072]{2,1,0:T(8,128)(2,1)S(1)} %bitcast.12, bf16[2,64,3072]{2,1,0:T(8,128)(2,1)S(1)} %collective-permute-done.1.ahead, bf16[2,64,3072]{2,1,0:T(8,128)(2,1)S(1)} %collective-permute-done.3.opposite, ...), custom_call_target="tpu_custom_call" | custom-call | tf_op jit(solution)/shard_map/pallas_call | solution.py:247
  90.7 8.0 %all_to_all.21.parts = f32[8,16,128]{2,1,0:T(8,128)S(1)} all-to-all(f32[8,16,128]{2,1,0:T(8,128)S(1)} %shard_map.116), channel_id=1, replica_groups=mesh['x'=4,'h'=2,'z1'=4,'z0'=2,'expert'=4,'tensor'=2] {'x','tensor'}, dimensions={0} | all-to-all | bytes 131072 | tf_op jit(solution)/shard_map/all_to_all | solution.py:185
  98.7 0.7 shard_map.117
  (5 shorter events, 0.0 us)
Async XLA Ops:
  0.6 3.9 %collective-permute-start = (bf16[64,512]{1,0:T(8,128)(2,1)}, bf16[64,512]{1,0:T(8,128)(2,1)S(1)}, u32[]{:S(2)}, u32[]{:S(2)}) collective-permute-start(bf16[64,512]{1,0:T(8,128)(2,1)} %bitcast.17), channel_id=1, source_target_pairs={{0,1},{1,0},{2,3},{3,2},{4,5},{5,4},{6,7},{7,6},{8,9},{9,8},{10,11... | collective-permute-start | bytes 196616 | tf_op jit(solution)/shard_map/ppermute | solution.py:192
  5.7 43.0 %copy-start = (bf16[1,2,64,3072]{3,2,1,0:T(8,128)(2,1)S(1)}, bf16[1,2,64,3072]{3,2,1,0:T(8,128)(2,1)}, u32[]{:S(2)}) copy-start(bf16[1,2,64,3072]{3,2,1,0:T(8,128)(2,1)} %param.15) | copy-start | bytes 2359300
  5.8 59.0 %copy-start.1 = (f32[2,1,1,6144]{3,2,1,0:T(1,128)S(1)}, f32[2,1,1,6144]{3,2,1,0:T(1,128)}, u32[]{:S(2)}) copy-start(f32[2,1,1,6144]{3,2,1,0:T(1,128)} %param.12) | copy-start | bytes 147460
  5.8 59.0 %copy-start.2 = (f32[2,1,1,6144]{3,2,1,0:T(1,128)S(1)}, f32[2,1,1,6144]{3,2,1,0:T(1,128)}, u32[]{:S(2)}) copy-start(f32[2,1,1,6144]{3,2,1,0:T(1,128)} %param.13) | copy-start | bytes 147460
  5.8 59.0 %copy-start.3 = (f32[2,1,1,6144]{3,2,1,0:T(1,128)S(1)}, f32[2,1,1,6144]{3,2,1,0:T(1,128)}, u32[]{:S(2)}) copy-start(f32[2,1,1,6144]{3,2,1,0:T(1,128)} %param.14) | copy-start | bytes 147460
  34.9 29.9 %all-to-all-start.1 = ((bf16[16,48,128]{2,1,0:T(8,128)(2,1)}), bf16[16,48,128]{2,1,0:T(8,128)(2,1)S(1)}, u32[]{:S(2)}, u32[]{:S(2)}) async-start(bf16[16,48,128]{2,1,0:T(8,128)(2,1)} %shard_map.113), calls=%async_computation.1 | async-start | bytes 393216 | tf_op jit(solution)/shard_map/all_to_all | solution.py:185
  48.8 21.5 %collective-permute-start.1 = (bf16[2,64,3072]{2,1,0:T(8,128)(2,1)S(1)}, bf16[2,64,3072]{2,1,0:T(8,128)(2,1)S(1)}, u32[]{:S(2)}, u32[]{:S(2)}) collective-permute-start(bf16[2,64,3072]{2,1,0:T(8,128)(2,1)S(1)} %bitcast.10), channel_id=1, source_target_pairs={{0,128},{1,385},{128,256},{129,1},{256,384},{257,129},{384,0},{385... | collective-permute-start | bytes 2359304 | tf_op jit(solution)/shard_map/ppermute | solution.py:181
  50.9 21.4 %collective-permute-start.2 = (bf16[2,64,3072]{2,1,0:T(8,128)(2,1)S(1)}, bf16[2,64,3072]{2,1,0:T(8,128)(2,1)S(1)}, u32[]{:S(2)}, u32[]{:S(2)}) collective-permute-start(bf16[2,64,3072]{2,1,0:T(8,128)(2,1)S(1)} %bitcast.11), channel_id=1, source_target_pairs={{0,384},{1,129},{128,0},{129,257},{256,128},{257,385},{384,256},{3... | collective-permute-start | bytes 2359304 | tf_op jit(solution)/shard_map/ppermute | solution.py:181
  66.2 23.1 %all-to-all-start.2 = ((bf16[32,48,128]{2,1,0:T(8,128)(2,1)}), bf16[32,48,128]{2,1,0:T(8,128)(2,1)S(1)}, u32[]{:S(2)}, u32[]{:S(2)}) async-start(bf16[32,48,128]{2,1,0:T(8,128)(2,1)} %get-tuple-element.24), calls=%async_computation.2 | async-start | bytes 786432 | tf_op jit(solution)/shard_map/all_to_all | solution.py:185
  70.3 19.3 %collective-permute-start.3 = (bf16[2,64,3072]{2,1,0:T(8,128)(2,1)S(1)}, bf16[2,64,3072]{2,1,0:T(8,128)(2,1)S(1)}, u32[]{:S(2)}, u32[]{:S(2)}) collective-permute-start(bf16[2,64,3072]{2,1,0:T(8,128)(2,1)S(1)} %collective-permute-done.1.ahead), channel_id=1, source_target_pairs={{0,128},{1,385},{128,256},{129,1},{256,384},{257,129},{384,0},{385... | collective-permute-start | bytes 2359304 | tf_op jit(solution)/shard_map/ppermute | solution.py:181

commit v5 on v4

--- a/solution.py
+++ b/solution.py
@@ -14,9 +14,9 @@
 weight_decay = 0.1
 adam_epsilon = 1e-08
 
-DP = ("x", "h", "z1", "z0")
-NEAR = ("x", "z0")
-FAR = ("tensor", "h", "z1")
+DP = ("x1", "x0", "h", "z1", "z0")
+PLANE = ("x1", "x0", "z1", "z0", "tensor")
+FAR = ("tensor", "x1", "h", "z1")
 LANES = 128
 COLS = 24
 BLOCK = 512
@@ -65,8 +65,9 @@
     me = lax.axis_index("tensor")
     i = lax.broadcasted_iota(jnp.int32, (256, 64), 0)
     c = lax.broadcasted_iota(jnp.int32, (256, 64), 1)
-    z1, h, t, z0, x = (i >> 1) & 3, (i >> 3) & 1, (i >> 4) & 1, (i >> 5) & 1, i >> 6
-    found = c == x * 16 + h * 8 + z1 * 2 + z0
+    z1, h, x1, t = (i >> 1) & 3, (i >> 3) & 1, (i >> 4) & 1, (i >> 5) & 1
+    z0, x0 = (i >> 6) & 1, i >> 7
+    found = c == x1 * 32 + x0 * 16 + h * 8 + z1 * 2 + z0
     picks = [jnp.where(found & (t == w), 1.0, 0.0).astype(jnp.bfloat16) for w in (me, 1 - me)]
     spread = jnp.dot(picks[0], mine[...], preferred_element_type=jnp.float32)
     spread += jnp.dot(picks[1], other[...], preferred_element_type=jnp.float32)
@@ -77,19 +78,19 @@
         ).astype(jnp.bfloat16)
         for j in range(GROUP):
             block = piece[:, j * LANES : (j + 1) * LANES]
-            out[:, k * GROUP + j] = block.reshape(8, 32, LANES)
+            out[:, k * GROUP + j] = block.reshape(4, 64, LANES)
 
 
 def near_sum_kernel(parts, out, total, ready, sems):
     copies = [
-        pltpu.make_async_copy(ready.at[pl.ds(k * 4, 4)], out.at[pl.ds(k * 4, 4)], sems.at[k])
+        pltpu.make_async_copy(ready.at[pl.ds(k * 8, 8)], out.at[pl.ds(k * 8, 8)], sems.at[k])
         for k in range(4)
     ]
     for j in range(COLS):
-        total[j * 32 : (j + 1) * 32] = jnp.sum(parts[:, j].astype(jnp.float32), axis=0)
+        total[j * 64 : (j + 1) * 64] = jnp.sum(parts[:, j].astype(jnp.float32), axis=0)
     for k in range(4):
-        for d in range(4 * k, 4 * k + 4):
-            pair = [total[pl.ds(2 * d + e, COLS, stride=32), :] for e in range(2)]
+        for d in range(8 * k, 8 * k + 8):
+            pair = [total[pl.ds(2 * d + e, COLS, stride=64), :] for e in range(2)]
             ready[d] = jnp.concatenate(pair, axis=0).astype(jnp.bfloat16)
         copies[k].start()
     for copy in copies:
@@ -104,7 +105,7 @@
         for t in range(2)
     ]
     for t in range(2):
-        grad = jnp.sum(parts[t * 8 : (t + 1) * 8].astype(jnp.float32), axis=0)
+        grad = jnp.sum(parts[t * 16 : (t + 1) * 16].astype(jnp.float32), axis=0)
         weights = []
         for e in range(2):
             at = (e, pl.ds(t * COLS, COLS), slice(None))
@@ -128,7 +129,7 @@
 
 
 def gate_kernel(weights, own, ahead, opposite, back, out):
-    me = lax.axis_index("x")
+    me = lax.axis_index("x1") * 2 + lax.axis_index("x0")
     step = 1 - 2 * lax.axis_index("tensor")
     inputs = (own, ahead, opposite, back)
     totals = []
@@ -178,7 +179,18 @@
     pairs = [
         (x * 2 + t, (x + (by if t == 0 else -by)) % 4 * 2 + t) for x in range(4) for t in range(2)
     ]
-    return lax.ppermute(array, ("x", "tensor"), pairs)
+    return lax.ppermute(array, ("x1", "x0", "tensor"), pairs)
+
+
+def squares():
+    found = []
+    for t in range(2):
+        for x in range(t, 4, 2):
+            for z in range(t, 8, 2):
+                xs = sorted((x, (x + 1) % 4), key=lambda i: i % 2)
+                zs = sorted((z, (z + 1) % 8), key=lambda i: i % 2)
+                found.append([(i * 8 + k) * 2 + t for i in xs for k in zs])
+    return found
 
 
 def swap(array, axes):
@@ -207,19 +219,19 @@
     )
     parts = call(
         grad_kernel,
-        pltpu.VMEM((8, COLS, 32, LANES), bf16),
+        pltpu.VMEM((4, COLS, 64, LANES), bf16),
         [VMEM] * 4,
     )(hidden, other, inside, held)
-    parts = swap(parts, NEAR)
+    parts = lax.all_to_all(parts, PLANE, 0, 0, tiled=True, axis_index_groups=squares())
     parts, inputs = lax.optimization_barrier((parts, next_rows[0]))
     ahead, back = shift(inputs, 1), shift(inputs, -1)
     parts = call(
         near_sum_kernel,
-        pltpu.HBM((16, 48, LANES), bf16),
+        pltpu.HBM((32, 48, LANES), bf16),
         [VMEM],
         [
-            pltpu.VMEM((COLS * 32, LANES), f32),
-            pltpu.VMEM((16, 48, LANES), bf16),
+            pltpu.VMEM((COLS * 64, LANES), f32),
+            pltpu.VMEM((32, 48, LANES), bf16),
             pltpu.SemaphoreType.DMA((4,)),
         ],
         out_specs=HBM,
@@ -247,14 +259,15 @@
     gates = call(gate_kernel, shape((8, 16, LANES), f32), [VMEM] * 5)(
         weights, inputs, ahead, opposite, back
     )
-    gates = swap(gates, ("x", "tensor"))
+    gates = swap(gates, ("x1", "x0", "tensor"))
     gates = call(end_kernel, shape((2, 64, 64), f32), [VMEM])(gates)
     return (*[a.reshape(2, 1, 1, 6144) for a in new], gates[None])
 
 
 def solution(mesh):
     fine = Mesh(
-        mesh.devices.reshape(4, 2, 4, 2, 4, 2), ("x", "h", "z1", "z0", "expert", "tensor")
+        mesh.devices.reshape(2, 2, 2, 4, 2, 4, 2),
+        ("x1", "x0", "h", "z1", "z0", "expert", "tensor"),
     )
     shard = P("expert", "tensor", DP, None)
     placed = (

time: 99.9 us -> 97.7 us (0.978)
  blocking collectives: 36 us -> 25.2 us
  waiting for transfers between devices: 26.1 us -> 31.5 us
  starting transfers between devices: 28.7 us -> 31.6 us
    all_to_all x2 -> x1, blocking collectives: 36 us -> 8 us  [swap(): return lax.all_to_all(array, axes, 0, 0, tiled=True)]
    all_to_all x0 -> x1, blocking collectives: none -> 17.2 us  [per_device(): lax.all_to_all(parts, PLANE, 0, 0, tiled=True, axis_index_groups=squares())]
    all_to_all x2, waiting for transfers between devices: 26 us -> 31.5 us  [swap(): return lax.all_to_all(array, axes, 0, 0, tiled=True)]
    all_to_all x2, starting transfers between devices: 17.8 us -> 20.2 us  [swap(): return lax.all_to_all(array, axes, 0, 0, tiled=True)]
  transfers between devices with their start and end apart: 6 -> 6, of which waited for: 3 -> 2; matrix products, arithmetic and copies ran while one was open for 0% -> 0% of each run, Pallas kernels for 4% -> 4%
where the time goes in v5:
time: 97.7 us; the launch traced here: 97.2 us
  starting transfers between devices  31.6 us (32%)
  waiting for transfers between devices  31.5 us (32%)
  blocking collectives  25.2 us (26%)
  Pallas kernels  8.01 us (8%)
    all_to_all x2, waiting for transfers between devices, swap(): return lax.all_to_all(array, axes, 0, 0, tiled=True)  31.5 us
    all_to_all x2, starting transfers between devices, swap(): return lax.all_to_all(array, axes, 0, 0, tiled=True)  20.2 us
    all_to_all x1, blocking collectives, per_device(): lax.all_to_all(parts, PLANE, 0, 0, tiled=True, axis_index_groups=squares())  17.2 us
    ppermute x3, starting transfers between devices, shift(): return lax.ppermute(array, ('x1', 'x0', 'tensor'), pairs)  9.44 us
    all_to_all x1, blocking collectives, swap(): return lax.all_to_all(array, axes, 0, 0, tiled=True)  8 us
    pallas_call x1, Pallas kernels, per_device(): call(stage_kernel, [pltpu.VMEM((512, 3072), bf16), pltpu.VMEM((64, 512),...  1.97 us
  transfers between devices with their start and end apart: 6, of which 2 were waited for; matrix products, arithmetic and copies ran while one was open for 0% of the time, Pallas kernels for 4%

profile of v5, /device:TPU:8, one launch (start us, length us, event | category | flops | bytes accessed | tf_op | source)
XLA Modules:
  0.0 97.2 jit_solution(3658519056880585284)
XLA Ops:
  0.6 1.9 %collective-permute-start = (bf16[64,512]{1,0:T(8,128)(2,1)}, bf16[64,512]{1,0:T(8,128)(2,1)S(1)}, u32[]{:S(2)}, u32[]{:S(2)}) collective-permute-start(bf16[64,512]{1,0:T(8,128)(2,1)} %bitcast.17), channel_id=1, source_target_pairs={{0,1},{1,0},{2,3},{3,2},{4,5},{5,4},{6,7},{7,6},{8,9},{9,8},{10,11... | collective-permute-start | bytes 196616 | tf_op jit(solution)/shard_map/ppermute | solution.py:204
  2.6 2.0 %shard_map.111 = (bf16[512,3072]{1,0:T(8,128)(2,1)S(1)}, bf16[64,512]{1,0:T(8,128)(2,1)S(1)}, bf16[256,512]{1,0:T(8,128)(2,1)S(1)}) custom-call(s32[1,2]{1,0:T(1,128)} %starts.1, s32[1,2]{1,0:T(1,128)} %sizes.1, bf16[64,512]{1,0:T(8,128)(2,1)} %bitcast.18, bf16[512,3072]{1,0:T(8,128)(2,1)} %bitcast.16), custom_call_target="tpu_custom_call" | custom-call | tf_op jit(solution)/shard_map/pallas_call | solution.py:205
  4.5 1.2 %shard_map.112 = bf16[4,24,64,128]{3,2,1,0:T(8,128)(2,1)S(1)} custom-call(bf16[64,512]{1,0:T(8,128)(2,1)S(1)} %get-tuple-element.15.mine, bf16[64,512]{1,0:T(8,128)(2,1)S(1)} %collective-permute-done.other, bf16[256,512]{1,0:T(8,128)(2,1)S(1)} %get-tuple-element.16.inside, bf16[512,3072]{1,0:T(8,128)(2,1)S(1)} %get-tuple-element.17.rows), custom_call_target="tpu_custom_call" | custom-call | tf_op jit(solution)/shard_map/pallas_call | solution.py:220
  5.8 0.0 copy-start
  5.8 0.0 copy-start.1
  5.8 0.0 copy-start.2
  5.8 0.0 copy-start.3
  5.8 17.2 %all_to_all.20.parts = bf16[4,24,64,128]{3,2,1,0:T(8,128)(2,1)S(1)} all-to-all(bf16[4,24,64,128]{3,2,1,0:T(8,128)(2,1)S(1)} %shard_map.112), channel_id=1, replica_groups={{0,8,128,136},{16,24,144,152},{32,40,160,168},{48,56,176,184},{256,264,..., dimensions={0} | all-to-all | bytes 3145728 | tf_op jit(solution)/shard_map/all_to_all | solution.py:225
  23.1 1.3 %shard_map.113 = bf16[32,48,128]{2,1,0:T(8,128)(2,1)} custom-call(bf16[4,24,64,128]{3,2,1,0:T(8,128)(2,1)S(1)} %all_to_all.20.parts), custom_call_target="tpu_custom_call" | custom-call | tf_op jit(solution)/shard_map/pallas_call | solution.py:228
  24.3 16.3 %all-to-all-start.1 = ((bf16[32,48,128]{2,1,0:T(8,128)(2,1)}), bf16[32,48,128]{2,1,0:T(8,128)(2,1)S(1)}, u32[]{:S(2)}, u32[]{:S(2)}) async-start(bf16[32,48,128]{2,1,0:T(8,128)(2,1)} %shard_map.113), calls=%async_computation.1 | async-start | bytes 786432 | tf_op jit(solution)/shard_map/all_to_all | solution.py:197
  40.7 2.4 %collective-permute-start.1 = (bf16[2,64,3072]{2,1,0:T(8,128)(2,1)S(1)}, bf16[2,64,3072]{2,1,0:T(8,128)(2,1)S(1)}, u32[]{:S(2)}, u32[]{:S(2)}) collective-permute-start(bf16[2,64,3072]{2,1,0:T(8,128)(2,1)S(1)} %bitcast.10), channel_id=1, source_target_pairs={{0,128},{1,385},{128,256},{129,1},{256,384},{257,129},{384,0},{385... | collective-permute-start | bytes 2359304 | tf_op jit(solution)/shard_map/ppermute | solution.py:182
  43.1 4.6 %collective-permute-start.2 = (bf16[2,64,3072]{2,1,0:T(8,128)(2,1)S(1)}, bf16[2,64,3072]{2,1,0:T(8,128)(2,1)S(1)}, u32[]{:S(2)}, u32[]{:S(2)}) collective-permute-start(bf16[2,64,3072]{2,1,0:T(8,128)(2,1)S(1)} %bitcast.11), channel_id=1, source_target_pairs={{0,384},{1,129},{128,0},{129,257},{256,128},{257,385},{384,256},{3... | collective-permute-start | bytes 2359304 | tf_op jit(solution)/shard_map/ppermute | solution.py:182
  47.8 15.5 %all-to-all-done.1.parts = bf16[32,48,128]{2,1,0:T(8,128)(2,1)S(1)} async-done(((bf16[32,48,128]{2,1,0:T(8,128)(2,1)}), bf16[32,48,128]{2,1,0:T(8,128)(2,1)S(1)}, u32[]{:S(2)}, u32[]{:S(2)}) %all-to-all-start.1) | async-done | bytes 393248 | tf_op jit(solution)/shard_map/all_to_all | solution.py:197
  63.3 1.5 %shard_map.114 = (f32[2,48,128]{2,1,0:T(8,128)}, f32[2,48,128]{2,1,0:T(8,128)}, f32[2,48,128]{2,1,0:T(8,128)}, bf16[32,48,128]{2,1,0:T(8,128)(2,1)}) custom-call(bf16[32,48,128]{2,1,0:T(8,128)(2,1)S(1)} %all-to-all-done.1.parts, f32[2,48,128]{2,1,0:T(8,128)S(1)} %bitcast.13, f32[2,48,128]{2,1,0:T(8,128)S(1)} %bitcast.14, f32[2,48,128]{2,1,0:T(8,128)S(1)} %bitcast.15), custom_call_target="tpu_custom_call" | custom-call | flops 3000000000 | tf_op jit(solution)/shard_map/pallas_call | solution.py:241
  64.7 3.9 %all-to-all-start.2 = ((bf16[32,48,128]{2,1,0:T(8,128)(2,1)}), bf16[32,48,128]{2,1,0:T(8,128)(2,1)S(1)}, u32[]{:S(2)}, u32[]{:S(2)}) async-start(bf16[32,48,128]{2,1,0:T(8,128)(2,1)} %get-tuple-element.24), calls=%async_computation.2 | async-start | bytes 786432 | tf_op jit(solution)/shard_map/all_to_all | solution.py:197
  68.6 0.0 collective-permute-done.1.ahead
  68.7 2.4 %collective-permute-start.3 = (bf16[2,64,3072]{2,1,0:T(8,128)(2,1)S(1)}, bf16[2,64,3072]{2,1,0:T(8,128)(2,1)S(1)}, u32[]{:S(2)}, u32[]{:S(2)}) collective-permute-start(bf16[2,64,3072]{2,1,0:T(8,128)(2,1)S(1)} %collective-permute-done.1.ahead), channel_id=1, source_target_pairs={{0,128},{1,385},{128,256},{129,1},{256,384},{257,129},{384,0},{385... | collective-permute-start | bytes 2359304 | tf_op jit(solution)/shard_map/ppermute | solution.py:182
  71.1 0.0 collective-permute-done.2.unused.back
  71.1 16.1 %all-to-all-done.2.got = bf16[32,48,128]{2,1,0:T(8,128)(2,1)S(1)} async-done(((bf16[32,48,128]{2,1,0:T(8,128)(2,1)}), bf16[32,48,128]{2,1,0:T(8,128)(2,1)S(1)}, u32[]{:S(2)}, u32[]{:S(2)}) %all-to-all-start.2) | async-done | bytes 393248 | tf_op jit(solution)/shard_map/all_to_all | solution.py:197
  87.1 0.3 shard_map.115.weights
  87.4 0.0 collective-permute-done.3.opposite
  87.4 1.1 %shard_map.116 = f32[8,16,128]{2,1,0:T(8,128)S(1)} custom-call(bf16[48,32,128]{2,1,0:T(8,128)(2,1)S(1)} %shard_map.115.weights, bf16[2,64,3072]{2,1,0:T(8,128)(2,1)S(1)} %bitcast.12, bf16[2,64,3072]{2,1,0:T(8,128)(2,1)S(1)} %collective-permute-done.1.ahead, bf16[2,64,3072]{2,1,0:T(8,128)(2,1)S(1)} %collective-permute-done.3.opposite, ...), custom_call_target="tpu_custom_call" | custom-call | tf_op jit(solution)/shard_map/pallas_call | solution.py:259
  88.5 8.0 %all_to_all.21.parts = f32[8,16,128]{2,1,0:T(8,128)S(1)} all-to-all(f32[8,16,128]{2,1,0:T(8,128)S(1)} %shard_map.116), channel_id=1, replica_groups=mesh['x1'=2,'x0'=2,'h'=2,'z1'=4,'z0'=2,'expert'=4,'tensor'=2] {'x1','x0'..., dimensions={0} | all-to-all | bytes 131072 | tf_op jit(solution)/shard_map/all_to_all | solution.py:197
  96.5 0.7 shard_map.117
  (5 shorter events, 0.0 us)
Async XLA Ops:
  0.6 3.9 %collective-permute-start = (bf16[64,512]{1,0:T(8,128)(2,1)}, bf16[64,512]{1,0:T(8,128)(2,1)S(1)}, u32[]{:S(2)}, u32[]{:S(2)}) collective-permute-start(bf16[64,512]{1,0:T(8,128)(2,1)} %bitcast.17), channel_id=1, source_target_pairs={{0,1},{1,0},{2,3},{3,2},{4,5},{5,4},{6,7},{7,6},{8,9},{9,8},{10,11... | collective-permute-start | bytes 196616 | tf_op jit(solution)/shard_map/ppermute | solution.py:204
  5.8 34.9 %copy-start = (bf16[1,2,64,3072]{3,2,1,0:T(8,128)(2,1)S(1)}, bf16[1,2,64,3072]{3,2,1,0:T(8,128)(2,1)}, u32[]{:S(2)}) copy-start(bf16[1,2,64,3072]{3,2,1,0:T(8,128)(2,1)} %param.15) | copy-start | bytes 2359300
  5.8 57.5 %copy-start.1 = (f32[2,1,1,6144]{3,2,1,0:T(1,128)S(1)}, f32[2,1,1,6144]{3,2,1,0:T(1,128)}, u32[]{:S(2)}) copy-start(f32[2,1,1,6144]{3,2,1,0:T(1,128)} %param.12) | copy-start | bytes 147460
  5.8 57.5 %copy-start.2 = (f32[2,1,1,6144]{3,2,1,0:T(1,128)S(1)}, f32[2,1,1,6144]{3,2,1,0:T(1,128)}, u32[]{:S(2)}) copy-start(f32[2,1,1,6144]{3,2,1,0:T(1,128)} %param.13) | copy-start | bytes 147460
  5.8 57.5 %copy-start.3 = (f32[2,1,1,6144]{3,2,1,0:T(1,128)S(1)}, f32[2,1,1,6144]{3,2,1,0:T(1,128)}, u32[]{:S(2)}) copy-start(f32[2,1,1,6144]{3,2,1,0:T(1,128)} %param.14) | copy-start | bytes 147460
  24.3 38.9 %all-to-all-start.1 = ((bf16[32,48,128]{2,1,0:T(8,128)(2,1)}), bf16[32,48,128]{2,1,0:T(8,128)(2,1)S(1)}, u32[]{:S(2)}, u32[]{:S(2)}) async-start(bf16[32,48,128]{2,1,0:T(8,128)(2,1)} %shard_map.113), calls=%async_computation.1 | async-start | bytes 786432 | tf_op jit(solution)/shard_map/all_to_all | solution.py:197
  40.7 27.9 %collective-permute-start.1 = (bf16[2,64,3072]{2,1,0:T(8,128)(2,1)S(1)}, bf16[2,64,3072]{2,1,0:T(8,128)(2,1)S(1)}, u32[]{:S(2)}, u32[]{:S(2)}) collective-permute-start(bf16[2,64,3072]{2,1,0:T(8,128)(2,1)S(1)} %bitcast.10), channel_id=1, source_target_pairs={{0,128},{1,385},{128,256},{129,1},{256,384},{257,129},{384,0},{385... | collective-permute-start | bytes 2359304 | tf_op jit(solution)/shard_map/ppermute | solution.py:182
  43.1 27.9 %collective-permute-start.2 = (bf16[2,64,3072]{2,1,0:T(8,128)(2,1)S(1)}, bf16[2,64,3072]{2,1,0:T(8,128)(2,1)S(1)}, u32[]{:S(2)}, u32[]{:S(2)}) collective-permute-start(bf16[2,64,3072]{2,1,0:T(8,128)(2,1)S(1)} %bitcast.11), channel_id=1, source_target_pairs={{0,384},{1,129},{128,0},{129,257},{256,128},{257,385},{384,256},{3... | collective-permute-start | bytes 2359304 | tf_op jit(solution)/shard_map/ppermute | solution.py:182
  64.7 22.4 %all-to-all-start.2 = ((bf16[32,48,128]{2,1,0:T(8,128)(2,1)}), bf16[32,48,128]{2,1,0:T(8,128)(2,1)S(1)}, u32[]{:S(2)}, u32[]{:S(2)}) async-start(bf16[32,48,128]{2,1,0:T(8,128)(2,1)} %get-tuple-element.24), calls=%async_computation.2 | async-start | bytes 786432 | tf_op jit(solution)/shard_map/all_to_all | solution.py:197
  68.7 18.7 %collective-permute-start.3 = (bf16[2,64,3072]{2,1,0:T(8,128)(2,1)S(1)}, bf16[2,64,3072]{2,1,0:T(8,128)(2,1)S(1)}, u32[]{:S(2)}, u32[]{:S(2)}) collective-permute-start(bf16[2,64,3072]{2,1,0:T(8,128)(2,1)S(1)} %collective-permute-done.1.ahead), channel_id=1, source_target_pairs={{0,128},{1,385},{128,256},{129,1},{256,384},{257,129},{384,0},{385... | collective-permute-start | bytes 2359304 | tf_op jit(solution)/shard_map/ppermute | solution.py:182

commit v6 on v5

--- a/solution.py
+++ b/solution.py
@@ -16,7 +16,7 @@
 
 DP = ("x1", "x0", "h", "z1", "z0")
 PLANE = ("x1", "x0", "z1", "z0", "tensor")
-FAR = ("tensor", "x1", "h", "z1")
+FAR = ("x1", "h", "z1")
 LANES = 128
 COLS = 24
 BLOCK = 512
@@ -65,7 +65,7 @@
     me = lax.axis_index("tensor")
     i = lax.broadcasted_iota(jnp.int32, (256, 64), 0)
     c = lax.broadcasted_iota(jnp.int32, (256, 64), 1)
-    z1, h, x1, t = (i >> 1) & 3, (i >> 3) & 1, (i >> 4) & 1, (i >> 5) & 1
+    t, z1, h, x1 = (i >> 1) & 1, (i >> 2) & 3, (i >> 4) & 1, (i >> 5) & 1
     z0, x0 = (i >> 6) & 1, i >> 7
     found = c == x1 * 32 + x0 * 16 + h * 8 + z1 * 2 + z0
     picks = [jnp.where(found & (t == w), 1.0, 0.0).astype(jnp.bfloat16) for w in (me, 1 - me)]
@@ -83,47 +83,59 @@
 
 def near_sum_kernel(parts, out, total, ready, sems):
     copies = [
-        pltpu.make_async_copy(ready.at[pl.ds(k * 8, 8)], out.at[pl.ds(k * 8, 8)], sems.at[k])
+        pltpu.make_async_copy(ready.at[pl.ds(k * 4, 4)], out.at[pl.ds(k * 4, 4)], sems.at[k])
         for k in range(4)
     ]
     for j in range(COLS):
         total[j * 64 : (j + 1) * 64] = jnp.sum(parts[:, j].astype(jnp.float32), axis=0)
     for k in range(4):
-        for d in range(8 * k, 8 * k + 8):
-            pair = [total[pl.ds(2 * d + e, COLS, stride=64), :] for e in range(2)]
+        for d in range(4 * k, 4 * k + 4):
+            pair = [total[pl.ds(4 * d + e, COLS, stride=64), :] for e in range(4)]
             ready[d] = jnp.concatenate(pair, axis=0).astype(jnp.bfloat16)
         copies[k].start()
     for copy in copies:
         copy.wait()
 
 
-def step_kernel(parts, master, first, second, new_master, new_first, new_second, send, block, sems):
-    copies = [
-        pltpu.make_async_copy(
-            block.at[pl.ds(t * 16, 16)], send.at[pl.ds(t * 16, 16)], sems.at[t]
-        )
-        for t in range(2)
-    ]
-    for t in range(2):
-        grad = jnp.sum(parts[t * 16 : (t + 1) * 16].astype(jnp.float32), axis=0)
-        weights = []
+def step_kernel(parts, near, far, new_near, new_far, send, block, sem):
+    me = lax.axis_index("tensor")
+    half = pl.ds(pl.multiple_of(me * COLS, COLS), COLS)
+    grad = jnp.sum(parts[...].astype(jnp.float32), axis=0)
+    mine = []
+    for state, new, t in ((near, new_near, 0), (far, new_far, 1)):
         for e in range(2):
-            at = (e, pl.ds(t * COLS, COLS), slice(None))
-            results = adamw(grad[e * COLS : (e + 1) * COLS], master[at], first[at], second[at])
-            new_master[at], new_first[at], new_second[at] = results
-            weights.append(results[0])
-        both = jnp.concatenate(weights, axis=0).astype(jnp.bfloat16)
-        for d in range(16):
-            block[t * 16 + d] = both
-        copies[t].start()
-    for copy in copies:
-        copy.wait()
+            low, high = (grad[(w * 2 + e) * COLS : (w * 2 + e + 1) * COLS] for w in range(2))
+            own = jnp.where(me == t, low, high)
+            results = adamw(own, *[state[2 * i + e, half, :] for i in range(3)])
+            for i in range(3):
+                new[2 * i + e] = results[i]
+            mine.append(results[0])
+    first = [jnp.where(me == 0, mine[e], mine[2 + e]) for e in range(2)]
+    second = [jnp.where(me == 0, mine[2 + e], mine[e]) for e in range(2)]
+    both = jnp.concatenate(first + second, axis=0).astype(jnp.bfloat16)
+    for d in range(16):
+        block[d] = both
+    copy = pltpu.make_async_copy(block, send, sem)
+    copy.start()
+    copy.wait()
+
+
+def join_kernel(near, far, *out):
+    me = lax.axis_index("tensor")
+    for part, t in ((near, me), (far, 1 - me)):
+        half = pl.ds(pl.multiple_of(t * COLS, COLS), COLS)
+        for i in range(3):
+            for e in range(2):
+                out[i][e, half, :] = part[2 * i + e]
 
 
 def turn_kernel(got, unused, out, wide):
     del unused
-    for r in range(32):
-        wide[r * 48 : (r + 1) * 48] = got[r].astype(jnp.float32)
+    for r in range(16):
+        for t in range(2):
+            row = t * 16 + r
+            at = pl.ds(t * 48, 48)
+            wide[row * 48 : (row + 1) * 48] = got[r, at, :].astype(jnp.float32)
     for k in range(48):
         out[k] = wide[pl.ds(k, 32, stride=48), :].astype(jnp.bfloat16)
 
@@ -227,28 +239,33 @@
     ahead, back = shift(inputs, 1), shift(inputs, -1)
     parts = call(
         near_sum_kernel,
-        pltpu.HBM((32, 48, LANES), bf16),
+        pltpu.HBM((16, 96, LANES), bf16),
         [VMEM],
         [
             pltpu.VMEM((COLS * 64, LANES), f32),
-            pltpu.VMEM((32, 48, LANES), bf16),
+            pltpu.VMEM((16, 96, LANES), bf16),
             pltpu.SemaphoreType.DMA((4,)),
         ],
         out_specs=HBM,
     )(parts)
     parts = swap(parts, FAR)
-    state = [a.reshape(2, 48, LANES) for a in (master, moment1, moment2)]
-    *new, send = call(
+    state = jnp.concatenate([a.reshape(2, 48, LANES) for a in (master, moment1, moment2)])
+    flip = [(0, 1), (1, 0)]
+    far_state = lax.ppermute(state, "tensor", flip)
+    new_near, new_far, send = call(
         step_kernel,
-        [shape((2, 48, LANES), f32)] * 3 + [pltpu.HBM((32, 48, LANES), bf16)],
-        [VMEM] * 4,
-        [pltpu.VMEM((32, 48, LANES), bf16), pltpu.SemaphoreType.DMA((2,))],
-        out_specs=[VMEM] * 3 + [HBM],
+        [shape((6, COLS, LANES), f32)] * 2 + [pltpu.HBM((16, 96, LANES), bf16)],
+        [VMEM] * 3,
+        [pltpu.VMEM((16, 96, LANES), bf16), pltpu.SemaphoreType.DMA],
+        out_specs=[VMEM] * 2 + [HBM],
         flops=LATE,
-    )(parts, *state)
-    got = swap(send, ("tensor", "h", "z1", "z0"))
-    relayed, new[0] = lax.optimization_barrier((ahead, new[0]))
+    )(parts, state, far_state)
+    got = swap(send, ("h", "z1", "z0"))
+    relayed, new_near = lax.optimization_barrier((ahead, new_near))
     opposite = shift(relayed, 1)
+    new = call(join_kernel, [shape((2, 48, LANES), f32)] * 3, [VMEM] * 2)(
+        new_near, lax.ppermute(new_far, "tensor", flip)
+    )
     weights = call(
         turn_kernel,
         shape((48, 32, LANES), bf16),

time: 97.7 us -> 97 us (level)
  blocking collectives: 25.2 us -> 17.2 us
  starting transfers between devices: 31.6 us -> 38.7 us
  waiting for transfers between devices: 31.5 us -> 28.6 us
  Pallas kernels: 8.01 us -> 9.61 us
  local copies, waits for them, and re-layouts: 0.03 us -> 1.27 us
    all_to_all x1 -> x0, blocking collectives: 8 us -> none  [swap(): return lax.all_to_all(array, axes, 0, 0, tiled=True)]
    ppermute x0 -> x2, starting transfers between devices: none -> 6.15 us  [the longest x1 4.23 us: per_device(): far_state = lax.ppermute(state, 'tensor', flip)]
    all_to_all x2 -> x3, waiting for transfers between devices: 31.5 us -> 28.6 us  [swap(): return lax.all_to_all(array, axes, 0, 0, tiled=True)]
    all_to_all x2 -> x3, starting transfers between devices: 20.2 us -> 23 us  [swap(): return lax.all_to_all(array, axes, 0, 0, tiled=True)]
    ppermute x3, starting transfers between devices: 9.44 us -> 7.71 us  [shift(): return lax.ppermute(array, ('x1', 'x0', 'tensor'), pairs)]
    unnamed x8 -> x14, local copies, waits for them, and re-layouts: 0.03 us -> 1.27 us
    pallas_call x2 -> x3, Pallas kernels: 2.76 us -> 3.71 us  [the longest x1 1.55 us: per_device(): call(join_kernel, [shape((2, 48, LANES), f32)] * 3, [VMEM] * 2)]
  transfers between devices with their start and end apart: 6 -> 9, of which waited for: 2 -> 3; matrix products, arithmetic and copies ran while one was open for 0% -> 0% of each run, Pallas kernels for 4% -> 7%
where the time goes in v6:
time: 97 us; the launch traced here: 96.4 us
  starting transfers between devices  38.7 us (40%)
  waiting for transfers between devices  28.6 us (29%)
  blocking collectives  17.2 us (18%)
  Pallas kernels  9.61 us (10%)
  local copies, waits for them, and re-layouts  1.27 us (1%)
    all_to_all x3, waiting for transfers between devices, swap(): return lax.all_to_all(array, axes, 0, 0, tiled=True)  28.6 us
    all_to_all x3, starting transfers between devices, swap(): return lax.all_to_all(array, axes, 0, 0, tiled=True)  23 us
    all_to_all x1, blocking collectives, per_device(): lax.all_to_all(parts, PLANE, 0, 0, tiled=True, axis_index_groups=squares())  17.2 us
    ppermute x3, starting transfers between devices, shift(): return lax.ppermute(array, ('x1', 'x0', 'tensor'), pairs)  7.71 us
    ppermute x1, starting transfers between devices, per_device(): far_state = lax.ppermute(state, 'tensor', flip)  4.23 us
    pallas_call x1, Pallas kernels, per_device(): call(stage_kernel, [pltpu.VMEM((512, 3072), bf16), pltpu.VMEM((64, 512),...  1.97 us
  transfers between devices with their start and end apart: 9, of which 3 were waited for; matrix products, arithmetic and copies ran while one was open for 0% of the time, Pallas kernels for 7%

profile of v6, /device:TPU:8, one launch (start us, length us, event | category | flops | bytes accessed | tf_op | source)
XLA Modules:
  0.0 96.4 jit_solution(17823294951094645827)
XLA Ops:
  0.6 1.9 %collective-permute-start = (bf16[64,512]{1,0:T(8,128)(2,1)}, bf16[64,512]{1,0:T(8,128)(2,1)S(1)}, u32[]{:S(2)}, u32[]{:S(2)}) collective-permute-start(bf16[64,512]{1,0:T(8,128)(2,1)} %bitcast.14), channel_id=1, source_target_pairs={{0,1},{1,0},{2,3},{3,2},{4,5},{5,4},{6,7},{7,6},{8,9},{9,8},{10,11... | collective-permute-start | bytes 196616 | tf_op jit(solution)/shard_map/ppermute | solution.py:216
  2.6 2.0 %shard_map.111 = (bf16[512,3072]{1,0:T(8,128)(2,1)S(1)}, bf16[64,512]{1,0:T(8,128)(2,1)S(1)}, bf16[256,512]{1,0:T(8,128)(2,1)S(1)}) custom-call(s32[1,2]{1,0:T(1,128)} %starts.1, s32[1,2]{1,0:T(1,128)} %sizes.1, bf16[64,512]{1,0:T(8,128)(2,1)} %bitcast.15, bf16[512,3072]{1,0:T(8,128)(2,1)} %bitcast.13), custom_call_target="tpu_custom_call" | custom-call | tf_op jit(solution)/shard_map/pallas_call | solution.py:217
  4.5 1.2 %shard_map.112 = bf16[4,24,64,128]{3,2,1,0:T(8,128)(2,1)S(1)} custom-call(bf16[64,512]{1,0:T(8,128)(2,1)S(1)} %get-tuple-element.17.mine, bf16[64,512]{1,0:T(8,128)(2,1)S(1)} %collective-permute-done.other, bf16[256,512]{1,0:T(8,128)(2,1)S(1)} %get-tuple-element.18.inside, bf16[512,3072]{1,0:T(8,128)(2,1)S(1)} %get-tuple-element.19.rows), custom_call_target="tpu_custom_call" | custom-call | tf_op jit(solution)/shard_map/pallas_call | solution.py:232
  5.8 0.0 copy-start.4
  5.8 17.2 %all_to_all.20.parts = bf16[4,24,64,128]{3,2,1,0:T(8,128)(2,1)S(1)} all-to-all(bf16[4,24,64,128]{3,2,1,0:T(8,128)(2,1)S(1)} %shard_map.112), channel_id=1, replica_groups={{0,8,128,136},{16,24,144,152},{32,40,160,168},{48,56,176,184},{256,264,..., dimensions={0} | all-to-all | bytes 3145728 | tf_op jit(solution)/shard_map/all_to_all | solution.py:237
  23.1 1.3 %shard_map.113 = bf16[16,96,128]{2,1,0:T(8,128)(2,1)} custom-call(bf16[4,24,64,128]{3,2,1,0:T(8,128)(2,1)S(1)} %all_to_all.20.parts), custom_call_target="tpu_custom_call" | custom-call | tf_op jit(solution)/shard_map/pallas_call | solution.py:240
  24.4 16.1 %all-to-all-start.1 = ((bf16[16,96,128]{2,1,0:T(8,128)(2,1)}), bf16[16,96,128]{2,1,0:T(8,128)(2,1)S(1)}, u32[]{:S(2)}, u32[]{:S(2)}) async-start(bf16[16,96,128]{2,1,0:T(8,128)(2,1)} %shard_map.113), calls=%async_computation.1 | async-start | bytes 786432 | tf_op jit(solution)/shard_map/all_to_all | solution.py:209
  40.4 2.2 %collective-permute-start.1 = (bf16[2,64,3072]{2,1,0:T(8,128)(2,1)S(1)}, bf16[2,64,3072]{2,1,0:T(8,128)(2,1)S(1)}, u32[]{:S(2)}, u32[]{:S(2)}) collective-permute-start(bf16[2,64,3072]{2,1,0:T(8,128)(2,1)S(1)} %bitcast.10), channel_id=1, source_target_pairs={{0,128},{1,385},{128,256},{129,1},{256,384},{257,129},{384,0},{385... | collective-permute-start | bytes 2359304 | tf_op jit(solution)/shard_map/ppermute | solution.py:194
  42.7 4.2 %collective-permute-start.2 = (f32[6,48,128]{2,1,0:T(8,128)S(1)}, f32[6,48,128]{2,1,0:T(8,128)S(1)}, u32[]{:S(2)}, u32[]{:S(2)}) collective-permute-start(f32[6,48,128]{2,1,0:T(8,128)S(1)} %pad_maximum_fusion.near), channel_id=1, source_target_pairs={{0,1},{1,0},{2,3},{3,2},{4,5},{5,4},{6,7},{7,6},{8,9},{9,8},{10,11... | collective-permute-start | bytes 442376 | tf_op jit(solution)/shard_map/ppermute | solution.py:254
  46.9 2.5 %collective-permute-start.4 = (bf16[2,64,3072]{2,1,0:T(8,128)(2,1)S(1)}, bf16[2,64,3072]{2,1,0:T(8,128)(2,1)S(1)}, u32[]{:S(2)}, u32[]{:S(2)}) collective-permute-start(bf16[2,64,3072]{2,1,0:T(8,128)(2,1)S(1)} %bitcast.11), channel_id=1, source_target_pairs={{0,384},{1,129},{128,0},{129,257},{256,128},{257,385},{384,256},{3... | collective-permute-start | bytes 2359304 | tf_op jit(solution)/shard_map/ppermute | solution.py:194
  49.5 13.4 %all-to-all-done.1.parts = bf16[16,96,128]{2,1,0:T(8,128)(2,1)S(1)} async-done(((bf16[16,96,128]{2,1,0:T(8,128)(2,1)}), bf16[16,96,128]{2,1,0:T(8,128)(2,1)S(1)}, u32[]{:S(2)}, u32[]{:S(2)}) %all-to-all-start.1) | async-done | bytes 393248 | tf_op jit(solution)/shard_map/all_to_all | solution.py:209
  62.8 0.9 shard_map.114
  63.7 0.6 copy-done.1
  64.4 0.6 copy-done.3
  65.0 3.6 %all-to-all-start.2 = ((bf16[16,96,128]{2,1,0:T(8,128)(2,1)}), bf16[16,96,128]{2,1,0:T(8,128)(2,1)S(1)}, u32[]{:S(2)}, u32[]{:S(2)}) async-start(bf16[16,96,128]{2,1,0:T(8,128)(2,1)} %get-tuple-element.28), calls=%async_computation.2 | async-start | bytes 786432 | tf_op jit(solution)/shard_map/all_to_all | solution.py:209
  68.6 3.0 %collective-permute-start.5 = (bf16[2,64,3072]{2,1,0:T(8,128)(2,1)S(1)}, bf16[2,64,3072]{2,1,0:T(8,128)(2,1)S(1)}, u32[]{:S(2)}, u32[]{:S(2)}) collective-permute-start(bf16[2,64,3072]{2,1,0:T(8,128)(2,1)S(1)} %collective-permute-done.1.ahead), channel_id=1, source_target_pairs={{0,128},{1,385},{128,256},{129,1},{256,384},{257,129},{384,0},{385... | collective-permute-start | bytes 2359304 | tf_op jit(solution)/shard_map/ppermute | solution.py:194
  71.5 1.9 %collective-permute-start.3 = (f32[6,24,128]{2,1,0:T(8,128)}, f32[6,24,128]{2,1,0:T(8,128)}, u32[]{:S(2)}, u32[]{:S(2)}) collective-permute-start(f32[6,24,128]{2,1,0:T(8,128)} %copy-done.3), channel_id=1, source_target_pairs={{0,1},{1,0},{2,3},{3,2},{4,5},{5,4},{6,7},{7,6},{8,9},{9,8},{10,11... | collective-permute-start | bytes 221192 | tf_op jit(solution)/shard_map/ppermute | solution.py:267
  73.5 11.3 %all-to-all-done.2.got = bf16[16,96,128]{2,1,0:T(8,128)(2,1)S(1)} async-done(((bf16[16,96,128]{2,1,0:T(8,128)(2,1)}), bf16[16,96,128]{2,1,0:T(8,128)(2,1)S(1)}, u32[]{:S(2)}, u32[]{:S(2)}) %all-to-all-start.2) | async-done | bytes 393248 | tf_op jit(solution)/shard_map/all_to_all | solution.py:209
  84.7 0.3 shard_map.116.weights
  85.0 1.7 %shard_map.117 = f32[8,16,128]{2,1,0:T(8,128)} custom-call(bf16[48,32,128]{2,1,0:T(8,128)(2,1)S(1)} %shard_map.116.weights, bf16[2,64,3072]{2,1,0:T(8,128)(2,1)S(1)} %bitcast.12, bf16[2,64,3072]{2,1,0:T(8,128)(2,1)S(1)} %collective-permute-done.1.ahead, bf16[2,64,3072]{2,1,0:T(8,128)(2,1)S(1)} %collective-permute-done.5.opposite, ...), custom_call_target="tpu_custom_call" | custom-call | tf_op jit(solution)/shard_map/pallas_call | solution.py:276
  86.8 3.4 %all-to-all-start.3 = ((f32[8,16,128]{2,1,0:T(8,128)}), f32[8,16,128]{2,1,0:T(8,128)S(1)}, u32[]{:S(2)}, u32[]{:S(2)}) async-start(f32[8,16,128]{2,1,0:T(8,128)} %shard_map.117), calls=%async_computation.3 | async-start | bytes 131072 | tf_op jit(solution)/shard_map/all_to_all | solution.py:209
  90.1 1.6 %shard_map.115 = (f32[2,48,128]{2,1,0:T(8,128)}, f32[2,48,128]{2,1,0:T(8,128)}, f32[2,48,128]{2,1,0:T(8,128)}) custom-call(f32[6,24,128]{2,1,0:T(8,128)S(1)} %copy-done.2, f32[6,24,128]{2,1,0:T(8,128)} %collective-permute-done.3.far), custom_call_target="tpu_custom_call" | custom-call | tf_op jit(solution)/shard_map/pallas_call | solution.py:266
  91.7 4.0 %all-to-all-done.3.parts = f32[8,16,128]{2,1,0:T(8,128)S(1)} async-done(((f32[8,16,128]{2,1,0:T(8,128)}), f32[8,16,128]{2,1,0:T(8,128)S(1)}, u32[]{:S(2)}, u32[]{:S(2)}) %all-to-all-start.3) | async-done | bytes 65568 | tf_op jit(solution)/shard_map/all_to_all | solution.py:209
  95.7 0.7 shard_map.118
  (18 shorter events, 0.1 us)
Async XLA Ops:
  0.6 3.9 %collective-permute-start = (bf16[64,512]{1,0:T(8,128)(2,1)}, bf16[64,512]{1,0:T(8,128)(2,1)S(1)}, u32[]{:S(2)}, u32[]{:S(2)}) collective-permute-start(bf16[64,512]{1,0:T(8,128)(2,1)} %bitcast.14), channel_id=1, source_target_pairs={{0,1},{1,0},{2,3},{3,2},{4,5},{5,4},{6,7},{7,6},{8,9},{9,8},{10,11... | collective-permute-start | bytes 196616 | tf_op jit(solution)/shard_map/ppermute | solution.py:216
  5.8 34.6 %copy-start = (bf16[1,2,64,3072]{3,2,1,0:T(8,128)(2,1)S(1)}, bf16[1,2,64,3072]{3,2,1,0:T(8,128)(2,1)}, u32[]{:S(2)}) copy-start(bf16[1,2,64,3072]{3,2,1,0:T(8,128)(2,1)} %param.15) | copy-start | bytes 2359300
  5.8 36.9 %copy-start.4 = (f32[2,1,1,6144]{3,2,1,0:T(1,128)S(1)}, f32[2,1,1,6144]{3,2,1,0:T(1,128)}, u32[]{:S(2)}) copy-start(f32[2,1,1,6144]{3,2,1,0:T(1,128)} %param.14) | copy-start | bytes 147460
  5.8 36.9 %copy-start.5 = (f32[2,1,1,6144]{3,2,1,0:T(1,128)S(1)}, f32[2,1,1,6144]{3,2,1,0:T(1,128)}, u32[]{:S(2)}) copy-start(f32[2,1,1,6144]{3,2,1,0:T(1,128)} %param.13) | copy-start | bytes 147460
  5.8 36.9 %copy-start.6 = (f32[2,1,1,6144]{3,2,1,0:T(1,128)S(1)}, f32[2,1,1,6144]{3,2,1,0:T(1,128)}, u32[]{:S(2)}) copy-start(f32[2,1,1,6144]{3,2,1,0:T(1,128)} %param.12) | copy-start | bytes 147460
  24.4 38.5 %all-to-all-start.1 = ((bf16[16,96,128]{2,1,0:T(8,128)(2,1)}), bf16[16,96,128]{2,1,0:T(8,128)(2,1)S(1)}, u32[]{:S(2)}, u32[]{:S(2)}) async-start(bf16[16,96,128]{2,1,0:T(8,128)(2,1)} %shard_map.113), calls=%async_computation.1 | async-start | bytes 786432 | tf_op jit(solution)/shard_map/all_to_all | solution.py:209
  40.4 28.1 %collective-permute-start.1 = (bf16[2,64,3072]{2,1,0:T(8,128)(2,1)S(1)}, bf16[2,64,3072]{2,1,0:T(8,128)(2,1)S(1)}, u32[]{:S(2)}, u32[]{:S(2)}) collective-permute-start(bf16[2,64,3072]{2,1,0:T(8,128)(2,1)S(1)} %bitcast.10), channel_id=1, source_target_pairs={{0,128},{1,385},{128,256},{129,1},{256,384},{257,129},{384,0},{385... | collective-permute-start | bytes 2359304 | tf_op jit(solution)/shard_map/ppermute | solution.py:194
  42.7 6.8 %collective-permute-start.2 = (f32[6,48,128]{2,1,0:T(8,128)S(1)}, f32[6,48,128]{2,1,0:T(8,128)S(1)}, u32[]{:S(2)}, u32[]{:S(2)}) collective-permute-start(f32[6,48,128]{2,1,0:T(8,128)S(1)} %pad_maximum_fusion.near), channel_id=1, source_target_pairs={{0,1},{1,0},{2,3},{3,2},{4,5},{5,4},{6,7},{7,6},{8,9},{9,8},{10,11... | collective-permute-start | bytes 442376 | tf_op jit(solution)/shard_map/ppermute | solution.py:254
  46.9 26.5 %collective-permute-start.4 = (bf16[2,64,3072]{2,1,0:T(8,128)(2,1)S(1)}, bf16[2,64,3072]{2,1,0:T(8,128)(2,1)S(1)}, u32[]{:S(2)}, u32[]{:S(2)}) collective-permute-start(bf16[2,64,3072]{2,1,0:T(8,128)(2,1)S(1)} %bitcast.11), channel_id=1, source_target_pairs={{0,384},{1,129},{128,0},{129,257},{256,128},{257,385},{384,256},{3... | collective-permute-start | bytes 2359304 | tf_op jit(solution)/shard_map/ppermute | solution.py:194
  63.7 0.6 copy-start.1
  64.3 0.6 copy-start.3
  65.0 19.8 %all-to-all-start.2 = ((bf16[16,96,128]{2,1,0:T(8,128)(2,1)}), bf16[16,96,128]{2,1,0:T(8,128)(2,1)S(1)}, u32[]{:S(2)}, u32[]{:S(2)}) async-start(bf16[16,96,128]{2,1,0:T(8,128)(2,1)} %get-tuple-element.28), calls=%async_computation.2 | async-start | bytes 786432 | tf_op jit(solution)/shard_map/all_to_all | solution.py:209
  68.6 16.5 %collective-permute-start.5 = (bf16[2,64,3072]{2,1,0:T(8,128)(2,1)S(1)}, bf16[2,64,3072]{2,1,0:T(8,128)(2,1)S(1)}, u32[]{:S(2)}, u32[]{:S(2)}) collective-permute-start(bf16[2,64,3072]{2,1,0:T(8,128)(2,1)S(1)} %collective-permute-done.1.ahead), channel_id=1, source_target_pairs={{0,128},{1,385},{128,256},{129,1},{256,384},{257,129},{384,0},{385... | collective-permute-start | bytes 2359304 | tf_op jit(solution)/shard_map/ppermute | solution.py:194
  71.5 18.6 %collective-permute-start.3 = (f32[6,24,128]{2,1,0:T(8,128)}, f32[6,24,128]{2,1,0:T(8,128)}, u32[]{:S(2)}, u32[]{:S(2)}) collective-permute-start(f32[6,24,128]{2,1,0:T(8,128)} %copy-done.3), channel_id=1, source_target_pairs={{0,1},{1,0},{2,3},{3,2},{4,5},{5,4},{6,7},{7,6},{8,9},{9,8},{10,11... | collective-permute-start | bytes 221192 | tf_op jit(solution)/shard_map/ppermute | solution.py:267
  85.0 5.1 %copy-start.2 = (f32[6,24,128]{2,1,0:T(8,128)S(1)}, f32[6,24,128]{2,1,0:T(8,128)}, u32[]{:S(2)}) copy-start(f32[6,24,128]{2,1,0:T(8,128)} %copy-done.1) | copy-start | bytes 221188
  86.8 8.9 %all-to-all-start.3 = ((f32[8,16,128]{2,1,0:T(8,128)}), f32[8,16,128]{2,1,0:T(8,128)S(1)}, u32[]{:S(2)}, u32[]{:S(2)}) async-start(f32[8,16,128]{2,1,0:T(8,128)} %shard_map.117), calls=%async_computation.3 | async-start | bytes 131072 | tf_op jit(solution)/shard_map/all_to_all | solution.py:209
